TPU v7x, 128 devices: a whole 4x4x4 slice. The times are simulated.
128 devices in a mesh: outer: 2 (over core), ep: 16 (over z, x), tp: 4 (over y).
Axes of the slice: x: 4, y: 4, z: 4, core: 2. Of those that a mesh axis runs over, the one named last changes fastest.
Arguments:
- tokens: bfloat16 [4096, 3584], P(('outer', 'ep')), may hold values from -27 to 27
- norm_gain: float32 [3584], replicated, may hold values from 0.5 to 1.5
- dense_weight: bfloat16 [3, 3584, 2560], P(None, 'outer', 'tp'), may hold values from -0.09375 to 0.09375
- expert_gate_up: bfloat16 [16, 2, 3584, 2560], P('ep', None, None, 'tp'), may hold values from -0.09375 to 0.09375
- expert_down: bfloat16 [16, 3584, 2560], P('ep', None, 'tp'), may hold values from -0.125 to 0.125
- expert_ids: int32 [4096, 2], P(('outer', 'ep')), may hold values from 0 to 15, all different within a row; in each aligned block of 128 rows (0 to 127, 128 to 255, ...) at most 24 rows name the same one
- gate_weights: float32 [4096, 2], P(('outer', 'ep')), may hold values from 0.1 to 1
- grad_out: bfloat16 [4096, 3584], P(('outer', 'ep')), may hold values from -6 to 6
Outputs:
- layer_out: bfloat16 [4096, 3584], P(('outer', 'ep'))
- grad_in: bfloat16 [4096, 3584], P(('outer', 'ep'))
Inputs may be any that keep to these rules, and one draw needn't show every extreme that they name: `expert_ids`: each row names two different experts. Of the 128 rows of one device at most 24 name any one expert, and in every draw some device has exactly 24 rows naming one expert.
All inputs are finite; a program needn't handle non-finite values.
Results may differ from a plain program's by a relative error of at most 0.009.
Values may be sent and summed in bfloat16 or wider, within the bound.
A program may use at most 128 MiB of HBM per device.

v0:
```python
import jax
import jax.numpy as jnp
from jax import lax
from jax.sharding import PartitionSpec as P


def silu_parts(values):
    sigmoid_v = jax.nn.sigmoid(values)
    return (values * sigmoid_v, sigmoid_v * (1.0 + values * (1.0 - sigmoid_v)))


def transpose_dot(left_side, right_side):
    return lax.dot_general(
        left_side, right_side, (((1,), (1,)), ((), ())), preferred_element_type=jnp.float32
    )


def slot_tables(expert_ids, expert_count, capacity, spill):
    tok_rows = expert_ids.shape[0]
    flat_ids = expert_ids.reshape(-1)
    onehot = (flat_ids[:, None] == jnp.arange(expert_count, dtype=jnp.int32)[None, :]).astype(
        jnp.int32
    )
    ranking = jnp.sum((jnp.cumsum(onehot, axis=0) - onehot) * onehot, axis=1)
    within = ranking < capacity
    token_of = jnp.arange(2 * tok_rows, dtype=jnp.int32) // 2
    local_at = jnp.where(within, flat_ids * capacity + ranking, expert_count * capacity)
    spill_at = jnp.where(within, expert_count * spill, flat_ids * spill + ranking - capacity)
    local_table = (
        jnp.full((expert_count * capacity,), tok_rows, jnp.int32)
        .at[local_at]
        .set(token_of, mode="drop")
    )
    spill_table = (
        jnp.full((expert_count * spill,), tok_rows, jnp.int32)
        .at[spill_at]
        .set(token_of, mode="drop")
    )
    answer_at = jnp.where(within, local_at, expert_count * capacity + spill_at)
    return (local_table, spill_table, answer_at)


def gather_rows(source, row_table, blocks, block_rows):
    padded = jnp.concatenate([source, jnp.zeros((1, source.shape[1]), source.dtype)], axis=0)
    return jnp.take(padded, row_table, axis=0).reshape(blocks, block_rows, source.shape[1])


def pod_blocks(local_rows, spill_rows, pod_count, own_pod, capacity):
    expert_count = local_rows.shape[0]
    filled = jnp.pad(spill_rows, ((0, 0), (0, capacity - spill_rows.shape[1]), (0, 0)))
    own_block = (jnp.arange(pod_count, dtype=jnp.int32) == own_pod)[:, None, None, None]
    stacked = jnp.where(own_block, local_rows[None], filled[None])
    return stacked.reshape(pod_count * expert_count, capacity, local_rows.shape[2])


def pick_blocks(received, pod_count, own_pod, spill):
    expert_count = received.shape[0] // pod_count
    split_up = received.reshape(pod_count, expert_count, received.shape[1], received.shape[2])
    got_local = lax.dynamic_index_in_dim(split_up, own_pod, 0, keepdims=False)
    got_spill = lax.dynamic_index_in_dim(split_up, 1 - own_pod, 0, keepdims=False)[:, :spill]
    return (got_local, got_spill)


def send_rows(local_rows, spill_rows, capacity, spill):
    pod_count = lax.axis_size("outer")
    own_pod = lax.axis_index("outer")
    joined = pod_blocks(local_rows, spill_rows, pod_count, own_pod, capacity)
    received = lax.all_to_all(joined, ("outer", "ep"), split_axis=0, concat_axis=0, tiled=True)
    got_local, got_spill = pick_blocks(received, pod_count, own_pod, spill)
    return (got_local, got_spill)


def return_rows(local_back, spill_back, capacity, spill):
    pod_count = lax.axis_size("outer")
    own_pod = lax.axis_index("outer")
    joined = pod_blocks(local_back, spill_back, pod_count, own_pod, capacity)
    received = lax.all_to_all(joined, ("outer", "ep"), split_axis=0, concat_axis=0, tiled=True)
    back_local, back_spill = pick_blocks(received, pod_count, own_pod, spill)
    return (back_local, back_spill)


def deliver(source, local_table, spill_table, expert_count, capacity, spill):
    local_rows = gather_rows(source, local_table, expert_count, capacity)
    spill_rows = gather_rows(source, spill_table, expert_count, spill)
    got_local, got_spill = send_rows(local_rows, spill_rows, capacity, spill)
    features = got_local.shape[2]
    return jnp.concatenate(
        [got_local.reshape(-1, features), got_spill.reshape(-1, features)], axis=0
    )


def answer(results, answer_at, gate_weights, expert_count, capacity, spill):
    features = results.shape[1]
    local_back = results[: expert_count * capacity].reshape(expert_count, capacity, features)
    spill_back = results[expert_count * capacity :].reshape(expert_count, spill, features)
    back_local, back_spill = return_rows(local_back, spill_back, capacity, spill)
    flat_back = jnp.concatenate(
        [back_local.reshape(-1, features), back_spill.reshape(-1, features)], axis=0
    )
    picked = (
        jnp.take(flat_back, answer_at, axis=0)
        .astype(jnp.float32)
        .reshape(gate_weights.shape[0], 2, features)
    )
    return jnp.sum(picked * gate_weights[:, :, None], axis=1)


def body(
    tokens, norm_gain, dense_weight, expert_gate_up, expert_down, expert_ids, gate_weights, grad_out
):
    expert_count = lax.axis_size("ep")
    tok_rows = tokens.shape[0]
    capacity = 2 * tok_rows // expert_count
    spill = max(2, capacity // 2)
    float_in = tokens.astype(jnp.float32)
    inverse = lax.rsqrt(jnp.mean(float_in * float_in, axis=1, keepdims=True) + 1e-05)
    normed = float_in * inverse
    hidden_in = (normed * norm_gain).astype(jnp.bfloat16)
    dense_full = lax.all_gather(dense_weight, "outer", axis=1, tiled=True)
    dense_gate = jnp.dot(hidden_in, dense_full[0], preferred_element_type=jnp.float32)
    dense_up = jnp.dot(hidden_in, dense_full[1], preferred_element_type=jnp.float32)
    dense_silu, dense_slope = silu_parts(dense_gate)
    dense_act = (dense_silu * dense_up).astype(jnp.bfloat16)
    dense_out = transpose_dot(dense_act, dense_full[2])
    local_table, spill_table, answer_at = slot_tables(expert_ids, expert_count, capacity, spill)
    gate_matrix = expert_gate_up[0, 0]
    up_matrix = expert_gate_up[0, 1]
    down_matrix = expert_down[0]
    rows_in = deliver(hidden_in, local_table, spill_table, expert_count, capacity, spill)
    expert_gate = jnp.dot(rows_in, gate_matrix, preferred_element_type=jnp.float32)
    expert_up = jnp.dot(rows_in, up_matrix, preferred_element_type=jnp.float32)
    expert_silu, expert_slope = silu_parts(expert_gate)
    expert_act = (expert_silu * expert_up).astype(jnp.bfloat16)
    pieces = transpose_dot(expert_act, down_matrix).astype(jnp.bfloat16)
    moe_out = answer(pieces, answer_at, gate_weights, expert_count, capacity, spill)
    summed_out = lax.psum((dense_out + moe_out).astype(jnp.bfloat16), "tp").astype(jnp.float32)
    layer_out = (float_in + summed_out).astype(jnp.bfloat16)
    dense_grad_act = jnp.dot(grad_out, dense_full[2], preferred_element_type=jnp.float32)
    dense_grad_gate = (dense_grad_act * dense_up * dense_slope).astype(jnp.bfloat16)
    dense_grad_up = (dense_grad_act * dense_silu).astype(jnp.bfloat16)
    dense_grad_in = transpose_dot(dense_grad_gate, dense_full[0]) + transpose_dot(
        dense_grad_up, dense_full[1]
    )
    rows_grad = deliver(grad_out, local_table, spill_table, expert_count, capacity, spill)
    expert_grad_act = jnp.dot(rows_grad, down_matrix, preferred_element_type=jnp.float32)
    expert_grad_gate = (expert_grad_act * expert_up * expert_slope).astype(jnp.bfloat16)
    expert_grad_up = (expert_grad_act * expert_silu).astype(jnp.bfloat16)
    grad_pieces = (
        transpose_dot(expert_grad_gate, gate_matrix) + transpose_dot(expert_grad_up, up_matrix)
    ).astype(jnp.bfloat16)
    moe_grad = answer(grad_pieces, answer_at, gate_weights, expert_count, capacity, spill)
    normed_grad = lax.psum(dense_grad_in + moe_grad, "tp")
    scaled = normed_grad * norm_gain
    project = jnp.mean(scaled * normed, axis=1, keepdims=True)
    grad_in = (grad_out.astype(jnp.float32) + inverse * (scaled - normed * project)).astype(
        jnp.bfloat16
    )
    return (layer_out, grad_in)


def solution(mesh):
    in_specs = (
        P(("outer", "ep"), None),
        P(),
        P(None, "outer", "tp"),
        P("ep", None, None, "tp"),
        P("ep", None, "tp"),
        P(("outer", "ep"), None),
        P(("outer", "ep"), None),
        P(("outer", "ep"), None),
    )
    out_specs = (P(("outer", "ep"), None), P(("outer", "ep"), None))
    return jax.shard_map(body, mesh=mesh, in_specs=in_specs, out_specs=out_specs, check_vma=False)
```

profile of v0, /device:TPU:0, one launch (start us, length us, event | category | flops | bytes accessed | tf_op | source)
XLA Modules:
  0.0 437.0 jit_solution(15190497413093814537)
XLA Ops:
  15.9 2.9 gather_fusion
  18.9 3.0 gather_fusion.3
  26.5 2.5 select_bitcast_fusion
  30.6 3.3 broadcast_select_fusion
  36.2 8.7 %all-to-all-start = ((bf16[32,16,3584]{2,1,0:T(8,128)(2,1)}), bf16[32,16,3584]{2,1,0:T(8,128)(2,1)}, u32[]{:S(2)}, u32[]{:S(2)}) async-start(bf16[32,16,3584]{2,1,0:T(8,128)(2,1)} %bitcast_select_fusion.3), calls=%async_computation | async-start | bytes 7340032 | tf_op jit(solution)/shard_map/all_to_all | solution.py:68
  45.0 48.3 %all-to-all-done = bf16[32,16,3584]{2,1,0:T(8,128)(2,1)} async-done(((bf16[32,16,3584]{2,1,0:T(8,128)(2,1)}), bf16[32,16,3584]{2,1,0:T(8,128)(2,1)}, u32[]{:S(2)}, u32[]{:S(2)}) %all-to-all-start) | async-done | bytes 3670048 | tf_op jit(solution)/shard_map/all_to_all | solution.py:68
  95.8 4.7 %fusion.11 = f32[384,640]{1,0:T(8,128)S(1)} fusion(bf16[1,2,3584,640]{3,2,1,0:T(8,128)(2,1)} %param.17, bf16[128,3584]{1,0:T(8,128)(2,1)S(1)} %slice_bitcast_fusion.14, bf16[256,3584]{1,0:T(8,128)(2,1)S(1)} %bitcast.110), kind=kOutput, calls=%fused_computation.26 | convolution fusion | flops 1767112704 | bytes 8323072 | tf_op jit(solution)/shard_map/dot_general | solution.py:130
  106.9 3.4 bitcast_select_fusion.2
  110.4 4.8 %all-to-all-start.2 = ((bf16[32,16,3584]{2,1,0:T(8,128)(2,1)}), bf16[32,16,3584]{2,1,0:T(8,128)(2,1)}, u32[]{:S(2)}, u32[]{:S(2)}) async-start(bf16[32,16,3584]{2,1,0:T(8,128)(2,1)} %get-tuple-element.26), calls=%async_computation.2 | async-start | bytes 7340032 | tf_op jit(solution)/shard_map/all_to_all | solution.py:68
  115.9 48.1 %all-to-all-done.2 = bf16[32,16,3584]{2,1,0:T(8,128)(2,1)} async-done(((bf16[32,16,3584]{2,1,0:T(8,128)(2,1)}), bf16[32,16,3584]{2,1,0:T(8,128)(2,1)}, u32[]{:S(2)}, u32[]{:S(2)}) %all-to-all-start.2) | async-done | bytes 3670048 | tf_op jit(solution)/shard_map/all_to_all | solution.py:68
  164.0 5.2 %all-to-all-start.1 = ((bf16[32,16,3584]{2,1,0:T(8,128)(2,1)}), bf16[32,16,3584]{2,1,0:T(8,128)(2,1)}, u32[]{:S(2)}, u32[]{:S(2)}) async-start(bf16[32,16,3584]{2,1,0:T(8,128)(2,1)} %get-tuple-element.25), calls=%async_computation.1 | async-start | bytes 7340032 | tf_op jit(solution)/shard_map/all_to_all | solution.py:77
  169.2 2.4 constant_dynamic-slice_fusion.1
  171.8 4.7 %fusion.3 = f32[384,640]{1,0:T(8,128)S(1)} fusion(bf16[1,3584,640]{2,1,0:T(8,128)(2,1)} %param.18, bf16[128,3584]{1,0:T(8,128)(2,1)S(1)} %slice_bitcast_fusion.11, bf16[256,3584]{1,0:T(8,128)(2,1)S(1)} %bitcast.112), kind=kOutput, calls=%fused_computation.18 | convolution fusion | flops 1767112704 | bytes 8323072 | tf_op jit(solution)/shard_map/dot_general | solution.py:145
  176.6 2.4 fusion.9
  183.9 34.1 %all-to-all-done.1 = bf16[32,16,3584]{2,1,0:T(8,128)(2,1)} async-done(((bf16[32,16,3584]{2,1,0:T(8,128)(2,1)}), bf16[32,16,3584]{2,1,0:T(8,128)(2,1)}, u32[]{:S(2)}, u32[]{:S(2)}) %all-to-all-start.1) | async-done | bytes 3670048 | tf_op jit(solution)/shard_map/all_to_all | solution.py:77
  218.0 4.8 %all-to-all-start.3 = ((bf16[32,16,3584]{2,1,0:T(8,128)(2,1)}), bf16[32,16,3584]{2,1,0:T(8,128)(2,1)}, u32[]{:S(2)}, u32[]{:S(2)}) async-start(bf16[32,16,3584]{2,1,0:T(8,128)(2,1)} %bitcast_select_fusion), calls=%async_computation.3 | async-start | bytes 7340032 | tf_op jit(solution)/shard_map/all_to_all | solution.py:77
  225.6 3.0 gather_fusion.2
  228.6 43.1 %all-to-all-done.3 = bf16[32,16,3584]{2,1,0:T(8,128)(2,1)} async-done(((bf16[32,16,3584]{2,1,0:T(8,128)(2,1)}), bf16[32,16,3584]{2,1,0:T(8,128)(2,1)}, u32[]{:S(2)}, u32[]{:S(2)}) %all-to-all-start.3) | async-done | bytes 3670048 | tf_op jit(solution)/shard_map/all_to_all | solution.py:77
  274.2 3.0 gather_fusion.5
  277.2 5.5 %select_convert_fusion.1 = (f32[256,3584]{1,0:T(8,128)}, f32[256,3584]{1,0:T(8,128)}) fusion(bf16[256,3584]{1,0:T(8,128)(2,1)} %gather_fusion.2, pred[256]{0:T(512)(128)(4,1)S(1)} %get-tuple-element.7, bf16[256,3584]{1,0:T(8,128)(2,1)} %gather_fusion.5), kind=kLoop, calls=%fused_computation.63 | loop fusion | flops 3670016 | bytes 11010304 | tf_op jit(solution)/shard_map/reshape | solution.py:103
  282.7 5.7 %reshape.233 = f32[128,2,3584]{2,1,0:T(2,128)} reshape(f32[256,3584]{1,0:T(8,128)} %get-tuple-element.23) | data formatting | bytes 7340032 | tf_op jit(solution)/shard_map/reshape | solution.py:103
  288.4 5.5 %reshape.235 = f32[128,2,3584]{2,1,0:T(2,128)} reshape(f32[256,3584]{1,0:T(8,128)} %get-tuple-element.24) | data formatting | bytes 7340032 | tf_op jit(solution)/shard_map/reshape | solution.py:103
  293.9 12.7 %multiply_reduce_fusion = (f32[128,3584]{1,0:T(8,128)S(1)}, f32[128,3584]{1,0:T(8,128)}) fusion(f32[128,2,3584]{2,1,0:T(2,128)} %reshape.235, f32[128,2]{1,0:T(8,128)S(1)} %copy.16, f32[128,2,3584]{2,1,0:T(2,128)} %reshape.233), kind=kLoop, calls=%fused_computation.40 | loop fusion | flops 2752512 | bytes 11011072 | tf_op jit(solution)/shard_map/reduce_sum | solution.py:105
  306.6 3.2 fusion.14
  309.8 3.3 fusion.15
  313.1 3.2 fusion.16
  316.3 3.9 fusion.13
  320.2 5.2 %fusion.1 = f32[128,3584]{1,0:T(8,128)} fusion(f32[128,3584]{1,0:T(8,128)S(1)} %get-tuple-element.4, f32[128,3584]{1,0:T(8,128)S(1)} %fusion.13, bf16[3,3584,640]{2,1,0:T(8,128)(2,1)} %all-gather.2.cloned.1.call-done, f32[128,640]{1,0:T(8,128)S(1)} %fusion.16, f32[128,640]{1,0:T(8,128)S(1)} %fusion.14), kind=kOutput, calls=%fused_computation.12 | convolution fusion | flops 588611584 | bytes 10747904 | tf_op jit(solution)/shard_map/dot_general | solution.py:13
  325.5 5.5 %fusion.2 = bf16[128,3584]{1,0:T(8,128)(2,1)} fusion(f32[128,3584]{1,0:T(8,128)} %get-tuple-element.6, bf16[3,3584,640]{2,1,0:T(8,128)(2,1)} %all-gather.2.cloned.1.call-done, f32[128,640]{1,0:T(8,128)S(1)} %fusion.15, f32[128,640]{1,0:T(8,128)S(1)} %fusion.14), kind=kOutput, calls=%fused_computation.14 | convolution fusion | flops 588611584 | bytes 7995392 | tf_op jit(solution)/shard_map/dot_general | solution.py:13
  331.0 47.7 %all-reduce.11.cloned.1.call-done = f32[128,3584]{1,0:T(8,128)} async-done(((f32[128,3584]{1,0:T(8,128)}), f32[128,3584]{1,0:T(8,128)}) %all-reduce.11.cloned.1.call-update) | async-done | bytes 1835024 | tf_op jit(solution)/shard_map/psum | solution.py:152
  380.8 45.8 %all-reduce.9.cloned.1.call-done = bf16[128,3584]{1,0:T(8,128)(2,1)} async-done(((bf16[128,3584]{1,0:T(8,128)(2,1)}), bf16[128,3584]{1,0:T(8,128)(2,1)}) %all-reduce.9.cloned.1.call-update) | async-done | bytes 917520 | tf_op jit(solution)/shard_map/psum | solution.py:136
  426.6 3.4 fusion.32
  (118 shorter events, 39.1 us)
Async XLA Ops:
  7.2 8.7 %copy-start.7 = (bf16[128,3584]{1,0:T(8,128)(2,1)S(1)}, bf16[128,3584]{1,0:T(8,128)(2,1)}, u32[]{:S(2)}) copy-start(bf16[128,3584]{1,0:T(8,128)(2,1)} %param.21) | copy-start | bytes 2752516
  14.8 0.9 copy-start.5
  26.5 4.1 copy-start.1
  30.6 3.3 copy-start.3
  36.2 8.7 %copy-start.9 = (bf16[16,8,3584]{2,1,0:T(8,128)(2,1)S(1)}, bf16[16,8,3584]{2,1,0:T(8,128)(2,1)}, u32[]{:S(2)}) copy-start(bf16[16,8,3584]{2,1,0:T(8,128)(2,1)} %get-tuple-element.29) | copy-start | bytes 2752516
  36.2 57.2 %all-to-all-start = ((bf16[32,16,3584]{2,1,0:T(8,128)(2,1)}), bf16[32,16,3584]{2,1,0:T(8,128)(2,1)}, u32[]{:S(2)}, u32[]{:S(2)}) async-start(bf16[32,16,3584]{2,1,0:T(8,128)(2,1)} %bitcast_select_fusion.3), calls=%async_computation | async-start | bytes 7340032 | tf_op jit(solution)/shard_map/all_to_all | solution.py:68
  95.7 4.9 %slice-start = ((s8[9175040]{0:T(1024)(128)(4,1)}), s8[4194304]{0:T(1024)(128)(4,1)S(1)}, s32[]{:S(2)}) async-start(s8[9175040]{0:T(1024)(128)(4,1)} %bitcast.116), calls=%async_computation.7 | async-start | bytes 8388608
  95.7 4.8 %slice-start.1 = ((s8[9175040]{0:T(1024)(128)(4,1)}), s8[4194304]{0:T(1024)(128)(4,1)S(1)}, s32[]{:S(2)}) async-start(s8[9175040]{0:T(1024)(128)(4,1)} %bitcast.116), calls=%async_computation.8 | async-start | bytes 8388608
  95.7 4.9 %slice-start.2 = ((s8[9175040]{0:T(1024)(128)(4,1)}), s8[786432]{0:T(1024)(128)(4,1)S(1)}, s32[]{:S(2)}) async-start(s8[9175040]{0:T(1024)(128)(4,1)} %bitcast.116), calls=%async_computation.9 | async-start | bytes 1572864
  95.8 7.2 %slice-start.6 = ((s8[4587520]{0:T(1024)(128)(4,1)}), s8[4194304]{0:T(1024)(128)(4,1)S(1)}, s32[]{:S(2)}) async-start(s8[4587520]{0:T(1024)(128)(4,1)} %bitcast.120), calls=%async_computation.13 | async-start | bytes 8388608
  100.6 2.3 copy-start.12
  100.6 2.3 slice-start.7
  103.0 2.4 copy-start.14
  105.4 1.5 copy-start.4
  110.4 53.7 %all-to-all-start.2 = ((bf16[32,16,3584]{2,1,0:T(8,128)(2,1)}), bf16[32,16,3584]{2,1,0:T(8,128)(2,1)}, u32[]{:S(2)}, u32[]{:S(2)}) async-start(bf16[32,16,3584]{2,1,0:T(8,128)(2,1)} %get-tuple-element.26), calls=%async_computation.2 | async-start | bytes 7340032 | tf_op jit(solution)/shard_map/all_to_all | solution.py:68
  115.2 191.4 %all-gather.2.cloned.1.call-start = ((), (), s32[]{:S(2)}) async-start(), calls=%async_computation.4 | async-start | bytes 20643840 | tf_op jit(solution)/shard_map/all_gather | solution.py:119
  164.0 12.5 %slice-start.3 = ((s8[9175040]{0:T(1024)(128)(4,1)}), s8[786432]{0:T(1024)(128)(4,1)S(1)}, s32[]{:S(2)}) async-start(s8[9175040]{0:T(1024)(128)(4,1)} %bitcast.118), calls=%async_computation.10 | async-start | bytes 1572864
  164.0 54.0 %all-to-all-start.1 = ((bf16[32,16,3584]{2,1,0:T(8,128)(2,1)}), bf16[32,16,3584]{2,1,0:T(8,128)(2,1)}, u32[]{:S(2)}, u32[]{:S(2)}) async-start(bf16[32,16,3584]{2,1,0:T(8,128)(2,1)} %get-tuple-element.25), calls=%async_computation.1 | async-start | bytes 7340032 | tf_op jit(solution)/shard_map/all_to_all | solution.py:77
  169.2 7.3 %slice-start.4 = ((s8[9175040]{0:T(1024)(128)(4,1)}), s8[4194304]{0:T(1024)(128)(4,1)S(1)}, s32[]{:S(2)}) async-start(s8[9175040]{0:T(1024)(128)(4,1)} %bitcast.118), calls=%async_computation.11 | async-start | bytes 8388608
  171.7 4.8 %slice-start.5 = ((s8[9175040]{0:T(1024)(128)(4,1)}), s8[4194304]{0:T(1024)(128)(4,1)S(1)}, s32[]{:S(2)}) async-start(s8[9175040]{0:T(1024)(128)(4,1)} %bitcast.118), calls=%async_computation.12 | async-start | bytes 8388608
  171.8 4.8 %copy-start.13 = (f32[384,640]{1,0:T(8,128)S(1)}, f32[384,640]{1,0:T(8,128)}, u32[]{:S(2)}) copy-start(f32[384,640]{1,0:T(8,128)} %copy-done.12) | copy-start | bytes 2949124
  171.8 4.8 %copy-start.15 = (f32[384,640]{1,0:T(8,128)S(1)}, f32[384,640]{1,0:T(8,128)}, u32[]{:S(2)}) copy-start(f32[384,640]{1,0:T(8,128)} %copy-done.14) | copy-start | bytes 2949124
  183.9 39.0 %copy-start.11 = (f32[128,2]{0,1:T(2,128)S(1)}, f32[128,2]{0,1:T(2,128)}, u32[]{:S(2)}) copy-start(f32[128,2]{0,1:T(2,128)} %param.20) | copy-start | bytes 3076
  218.0 53.7 %all-to-all-start.3 = ((bf16[32,16,3584]{2,1,0:T(8,128)(2,1)}), bf16[32,16,3584]{2,1,0:T(8,128)(2,1)}, u32[]{:S(2)}, u32[]{:S(2)}) async-start(bf16[32,16,3584]{2,1,0:T(8,128)(2,1)} %bitcast_select_fusion), calls=%async_computation.3 | async-start | bytes 7340032 | tf_op jit(solution)/shard_map/all_to_all | solution.py:77
  222.8 155.8 %all-reduce.11.cloned.1.call-start = ((), (), s32[]{:S(2)}) async-start(), calls=%async_computation.6 | async-start | bytes 3670016 | tf_op jit(solution)/shard_map/psum | solution.py:152
  293.9 12.7 %copy-start.6 = (bf16[128,3584]{1,0:T(8,128)(2,1)S(1)}, bf16[128,3584]{1,0:T(8,128)(2,1)}, u32[]{:S(2)}) copy-start(bf16[128,3584]{1,0:T(8,128)(2,1)} %copy-done.5) | copy-start | bytes 2752516
  309.8 3.3 copy-start.8
  325.4 101.2 %all-reduce.9.cloned.1.call-start = ((), (), s32[]{:S(2)}) async-start(), calls=%async_computation.5 | async-start | bytes 1835008 | tf_op jit(solution)/shard_map/psum | solution.py:136
  325.4 53.2 %copy-start = (bf16[128,3584]{1,0:T(8,128)(2,1)S(1)}, bf16[128,3584]{1,0:T(8,128)(2,1)}, u32[]{:S(2)}) copy-start(bf16[128,3584]{1,0:T(8,128)(2,1)} %param.14) | copy-start | bytes 2752516
  325.5 53.2 %copy-start.10 = (f32[3584]{0:T(1024)S(1)}, f32[3584]{0:T(1024)}, u32[]{:S(2)}) copy-start(f32[3584]{0:T(1024)} %param.15) | copy-start | bytes 43012
  378.7 47.9 %copy-start.2 = (f32[128,3584]{1,0:T(8,128)S(1)}, f32[128,3584]{1,0:T(8,128)}, u32[]{:S(2)}) copy-start(f32[128,3584]{1,0:T(8,128)} %all-reduce.11.cloned.1.call-done) | copy-start | bytes 5505028
Sparse Core Ops, SparseCore 0:
  117.7 29.6 all-gather.1
  325.5 53.1 all-reduce.10
  381.6 44.8 all-reduce.8
where the time goes:
time: 444 us; the launch traced here: 437 us
  waiting for transfers between devices  268 us (60%)
  local copies, waits for them, and re-layouts  45.6 us (10%)
  matrix products  43 us (10%)
  other arithmetic  42.2 us (10%)
  starting transfers between devices  23.6 us (5%)
  between operations  14.8 us (3%)
    all_to_all x2, waiting for transfers between devices, send_rows(): lax.all_to_all(joined, ('outer', 'ep'), split_axis=0, concat_axis=0, tile...  96.4 us
    all_to_all x2, waiting for transfers between devices, return_rows(): lax.all_to_all(joined, ('outer', 'ep'), split_axis=0, concat_axis=0, tile...  77.1 us
    psum x1, waiting for transfers between devices, body(): normed_grad = lax.psum(dense_grad_in + moe_grad, 'tp')  47.7 us
    psum x1, waiting for transfers between devices, body(): lax.psum((dense_out + moe_out).astype(jnp.bfloat16), 'tp')  45.8 us
    dot_general x6, matrix products, transpose_dot(): lax.dot_general(left_side, right_side, (((1,), (1,)), ((), ())), preferre...  21.6 us
    all_to_all x2, starting transfers between devices, send_rows(): lax.all_to_all(joined, ('outer', 'ep'), split_axis=0, concat_axis=0, tile...  13.5 us
    reduce_sum x1, other arithmetic, answer(): return jnp.sum(picked * gate_weights[:, :, None], axis=1)  12.7 us
    reshape x2, local copies, waits for them, and re-layouts, answer(): picked = jnp.take(flat_back, answer_at, axis=0).astype(jnp.float32).resha...  11.2 us
  transfers between devices with their start and end apart: 7, of which 6 were waited for; matrix products, arithmetic and copies ran while one was open for 14% of the time, Pallas kernels for 0%

commit v1 on v0

v1 whole, which is shorter than its diff:
```python
import jax
import jax.numpy as jnp
from jax import lax
from jax.experimental import pallas as pl
from jax.experimental.pallas import tpu as pltpu
from jax.sharding import PartitionSpec as P

MESH = pl.DeviceIdType.MESH
F32 = jnp.float32
BF16 = jnp.bfloat16
ROWS = 128
D = 3584
FF = 640
EP = 16
TP = 4
MOST = 24
SLOTS = EP * MOST
QUARTER = D // TP
HALF = D // 2
OWN = ROWS // TP
CHUNK = 256
EPS = 1e-05
STEPS = [(dz, dx) for dz in (0, 1, 3, 2) for dx in range(4) if (dz, dx) != (0, 0)]
GROUPS = (0, 1, 3, 2)


def silu_parts(values):
    sigmoid_v = jax.nn.sigmoid(values)
    return (values * sigmoid_v, sigmoid_v * (1.0 + values * (1.0 - sigmoid_v)))


def dot(left, right):
    return jnp.dot(left, right, preferred_element_type=F32)


def dot_t(left, right):
    return lax.dot_general(left, right, (((1,), (1,)), ((), ())), preferred_element_type=F32)


def kernel(
    tok, gain, dense_hbm, gate_up_hbm, down_hbm, ids, weights, grad,
    layer_out, grad_in,
    dense_w, gate_up, down, hid, send_h, send_g, rows_h, rows_g, mat_x,
    acc_gate, acc_up, acc_grad, act, dense_out, dense_grad,
    piece_o, piece_g, back_o, back_g, part_o, part_g, red_o, red_g, total_g,
    pick_hi, pick_lo,
    load_sem, core_s, core_r, disp_s, disp_r, ring_s, ring_r, fwd_s, fwd_r,
    self_sem, ret_s, ret_r, red_s, red_r, gat_s, gat_r,
):
    pod, me, tp = lax.axis_index("outer"), lax.axis_index("ep"), lax.axis_index("tp")
    z, x = me // 4, lax.rem(me, 4)
    right, left = lax.rem(tp + 1, TP), lax.rem(tp + 3, TP)

    def expert_at(dz, dx):
        return lax.rem(z + dz + 4, 4) * 4 + lax.rem(x + dx + 4, 4)

    barrier = pltpu.get_barrier_semaphore()
    for dz, dx in STEPS:
        pl.semaphore_signal(barrier, inc=1, device_id=(pod, expert_at(dz, dx), tp), device_id_type=MESH)
    for d in (1, 2, 3):
        pl.semaphore_signal(barrier, inc=1, device_id=(pod, me, lax.rem(tp + d, TP)), device_id_type=MESH)
    pl.semaphore_signal(barrier, inc=1, device_id=(1 - pod, me, tp), device_id_type=MESH)

    loads = [
        pltpu.make_async_copy(gate_up_hbm.at[0], gate_up, load_sem.at[0]),
        pltpu.make_async_copy(down_hbm.at[0], down, load_sem.at[1]),
    ]
    own_rows = pl.ds(pl.multiple_of(pod * HALF, HALF), HALF)
    other_rows = pl.ds(pl.multiple_of((1 - pod) * HALF, HALF), HALF)
    dense_loads = [
        pltpu.make_async_copy(dense_hbm.at[i], dense_w.at[i, own_rows], load_sem.at[2 + i])
        for i in range(3)
    ]
    for load in loads + dense_loads:
        load.start()

    float_in = tok[...].astype(F32)
    inverse = lax.rsqrt(jnp.mean(float_in * float_in, axis=1, keepdims=True) + EPS)
    hid[...] = (float_in * inverse * gain[...]).astype(BF16)

    lanes = lax.broadcasted_iota(jnp.int32, (ROWS, EP), 1)
    first = (ids[:, 0:1] == lanes).astype(F32)
    second = (ids[:, 1:2] == lanes).astype(F32)
    named = first + second
    below = (
        lax.broadcasted_iota(jnp.int32, (ROWS, ROWS), 0)
        > lax.broadcasted_iota(jnp.int32, (ROWS, ROWS), 1)
    ).astype(F32).astype(BF16)
    rank = dot(below, named.astype(BF16))
    slot = lax.broadcasted_iota(jnp.int32, (EP, SLOTS), 1)
    low = lax.broadcasted_iota(jnp.int32, (EP, SLOTS), 0) * MOST
    spread = ((slot >= low) & (slot < low + MOST)).astype(F32).astype(BF16)
    slot_f = lax.broadcasted_iota(jnp.int32, (ROWS, SLOTS), 1).astype(F32)
    within = slot_f - MOST * jnp.floor((slot_f + 0.5) * (1.0 / MOST))
    named_at = dot(named.astype(BF16), spread)
    rank_at = dot(rank.astype(BF16), spread)
    chosen = jnp.where((named_at > 0.5) & (jnp.abs(rank_at - within) < 0.5), 1.0, 0.0)
    weight = first * weights[:, 0:1] + second * weights[:, 1:2]
    weight_hi = weight.astype(BF16)
    weight_lo = (weight - weight_hi.astype(F32)).astype(BF16)
    pick_hi[...] = (chosen * dot(weight_hi, spread)).astype(BF16)
    pick_lo[...] = (chosen * dot(weight_lo, spread)).astype(BF16)
    gather = jnp.transpose(chosen).astype(BF16)

    quarter = pl.ds(pl.multiple_of(tp * QUARTER, 128), QUARTER)
    send_h[...] = dot(gather, hid[:, quarter]).reshape(EP, MOST, QUARTER).astype(BF16)

    def remote(src, dst, send, recv, device):
        return pltpu.make_async_remote_copy(
            src_ref=src, dst_ref=dst, send_sem=send, recv_sem=recv, device_id=device, device_id_type=MESH
        )

    def dispatch(a, send, rows):
        out = []
        for i, (dz, dx) in enumerate(STEPS):
            peer = expert_at(dz, dx)
            out.append(remote(send.at[peer], rows.at[tp, me], disp_s.at[a, i], disp_r.at[a, i], (pod, peer, tp)))
        for copy in out:
            copy.start()
        own = pltpu.make_async_copy(send.at[me], rows.at[tp, me], self_sem.at[a])
        own.start()
        return out, own

    pl.semaphore_wait(barrier, len(STEPS) + 4)
    sent_h, own_h = dispatch(0, send_h, rows_h)
    sent_core = [
        remote(dense_hbm.at[i], dense_w.at[i, own_rows], core_s.at[i], core_r.at[i], (1 - pod, me, tp))
        for i in range(3)
    ]
    for copy in sent_core:
        copy.start()
    send_g[...] = dot(gather, grad[:, quarter]).reshape(EP, MOST, QUARTER).astype(BF16)
    sent_g, own_g = dispatch(1, send_g, rows_g)

    def group_of(rows, q, dz):
        at = pl.multiple_of(lax.rem(z - dz + 4, 4) * 4, 4)
        return rows.at[q, pl.ds(at, 4)]

    def ring_out(a, rows, own):
        out = []
        own.wait()
        for n, group in enumerate(GROUPS):
            for i, (dz, dx) in enumerate(STEPS):
                if dz == group:
                    landed = rows.at[tp, expert_at(-dz, -dx)]
                    remote(landed, landed, disp_s.at[a, i], disp_r.at[a, i], (pod, expert_at(-dz, -dx), tp)).wait_recv()
            block = group_of(rows, tp, group)
            for way, peer in ((0, right), (1, left)):
                copy = remote(block, block, ring_s.at[a, way, n], ring_r.at[a, way, n], (pod, me, peer))
                copy.start()
                out.append(copy)
        return out

    def ring_on(a, rows):
        out = []
        for n, group in enumerate(GROUPS):
            for way, source, peer in ((0, left, right), (1, right, left)):
                block = group_of(rows, source, group)
                remote(block, block, ring_s.at[a, way, n], ring_r.at[a, way, n], (pod, me, source)).wait_recv()
                if n // 2 == way:
                    copy = remote(block, block, fwd_s.at[a, way, n % 2], fwd_r.at[a, way, n % 2], (pod, me, peer))
                    copy.start()
                    out.append(copy)
        return out

    def ring_end(a, rows):
        far = lax.rem(tp + 2, TP)
        for n, group in enumerate(GROUPS):
            way = n // 2
            block = group_of(rows, far, group)
            remote(block, block, fwd_s.at[a, way, n % 2], fwd_r.at[a, way, n % 2], (pod, me, far)).wait_recv()

    def pack(rows, q):
        def step(i, carry):
            block = rows[q, pl.ds(2 * i, 2)]
            mat_x[pl.ds(pl.multiple_of(i * 2 * MOST, 16), 2 * MOST), :] = (
                block.astype(F32).reshape(2 * MOST, QUARTER).astype(BF16)
            )
            return carry

        lax.fori_loop(0, EP // 2, step, 0)

    def forward_quarter(q, start):
        pack(rows_h, q)
        at = pl.ds(pl.multiple_of(q * QUARTER, QUARTER), QUARTER)
        if start:
            acc_gate[...] = dot(mat_x[...], gate_up[0, at, :])
            acc_up[...] = dot(mat_x[...], gate_up[1, at, :])
        else:
            acc_gate[...] += dot(mat_x[...], gate_up[0, at, :])
            acc_up[...] += dot(mat_x[...], gate_up[1, at, :])

    def backward_quarter(q, start):
        pack(rows_g, q)
        at = pl.ds(pl.multiple_of(q * QUARTER, QUARTER), QUARTER)
        if start:
            acc_grad[...] = dot(mat_x[...], down[at, :])
        else:
            acc_grad[...] += dot(mat_x[...], down[at, :])

    ring_h = ring_out(0, rows_h, own_h)
    for load in loads:
        load.wait()
    forward_quarter(tp, True)
    on_h = ring_on(0, rows_h)
    ring_g = ring_out(1, rows_g, own_g)
    forward_quarter(left, False)
    forward_quarter(right, False)
    ring_end(0, rows_h)
    forward_quarter(lax.rem(tp + 2, TP), False)

    silu, slope = silu_parts(acc_gate[...])
    act[0] = (silu * acc_up[...]).astype(BF16)

    def send_back(a, c, piece, back):
        out = []
        for i, (dz, dx) in enumerate(STEPS):
            peer = expert_at(dz, dx)
            out.append(
                remote(piece.at[c, peer], back.at[c, me], ret_s.at[a, c, i], ret_r.at[a, c, i], (pod, peer, tp))
            )
        for copy in out:
            copy.start()
        own = pltpu.make_async_copy(piece.at[c, me], back.at[c, me], self_sem.at[2 + 2 * a + c])
        own.start()
        return out, own

    def columns(c, n):
        return pl.ds(pl.multiple_of(c * HALF + n * CHUNK, CHUNK), CHUNK)

    def within_half(n):
        return pl.ds(pl.multiple_of(n * CHUNK, CHUNK), CHUNK)

    returned_o = []
    for c in range(2):
        def out_step(n, carry):
            piece = dot_t(act[0], down[columns(c, n), :])
            piece_o[c, :, :, within_half(n)] = piece.reshape(EP, MOST, CHUNK).astype(BF16)
            return carry

        lax.fori_loop(0, HALF // CHUNK, out_step, 0)
        returned_o.append(send_back(0, c, piece_o, back_o))

    on_g = ring_on(1, rows_g)

    for load in dense_loads:
        load.wait()
    for i in range(3):
        landed = dense_w.at[i, other_rows]
        remote(dense_hbm.at[i], landed, core_s.at[i], core_r.at[i], (1 - pod, me, tp)).wait_recv()

    wide = 512

    def dense_in_step(n, carry):
        gate, up, back = carry
        at = pl.ds(pl.multiple_of(n * wide, wide), wide)
        gate = gate + dot(hid[:, at], dense_w[0, at, :])
        up = up + dot(hid[:, at], dense_w[1, at, :])
        back = back + dot(grad[:, at], dense_w[2, at, :])
        return gate, up, back

    zeros = jnp.zeros((ROWS, FF), F32)
    d_gate, d_up, d_back = lax.fori_loop(0, D // wide, dense_in_step, (zeros, zeros, zeros))
    d_silu, d_slope = silu_parts(d_gate)
    d_act = (d_silu * d_up).astype(BF16)
    d_grad_gate = (d_back * d_up * d_slope).astype(BF16)
    d_grad_up = (d_back * d_silu).astype(BF16)

    def dense_out_step(n, carry):
        at = pl.ds(pl.multiple_of(n * CHUNK, CHUNK), CHUNK)
        dense_out[:, at] = dot_t(d_act, dense_w[2, at, :])
        dense_grad[:, at] = dot_t(d_grad_gate, dense_w[0, at, :]) + dot_t(d_grad_up, dense_w[1, at, :])
        return carry

    lax.fori_loop(0, D // CHUNK, dense_out_step, 0)

    backward_quarter(tp, True)
    backward_quarter(left, False)
    backward_quarter(right, False)
    ring_end(1, rows_g)
    backward_quarter(lax.rem(tp + 2, TP), False)
    silu, slope = silu_parts(acc_gate[...])
    act[0] = (acc_grad[...] * acc_up[...] * slope).astype(BF16)
    act[1] = (acc_grad[...] * silu).astype(BF16)
    for copies, own in returned_o:
        for copy in copies:
            copy.wait_send()
    returned_g = []
    for c in range(2):
        def grad_step(n, carry):
            at = columns(c, n)
            piece = dot_t(act[0], gate_up[0, at, :]) + dot_t(act[1], gate_up[1, at, :])
            piece_g[c, :, :, within_half(n)] = piece.reshape(EP, MOST, CHUNK).astype(BF16)
            return carry

        lax.fori_loop(0, HALF // CHUNK, grad_step, 0)
        returned_g.append(send_back(1, c, piece_g, back_g))

    mine = pl.ds(pl.multiple_of(tp * OWN, OWN), OWN)

    def combine(a, c, returned, back, dense, part, red):
        returned[c][1].wait()
        for i, (dz, dx) in enumerate(STEPS):
            source = expert_at(-dz, -dx)
            landed = back.at[c, source]
            remote(landed, landed, ret_s.at[a, c, i], ret_r.at[a, c, i], (pod, source, tp)).wait_recv()

        def step(n, carry):
            rows = back[c, :, :, within_half(n)].astype(F32).reshape(SLOTS, CHUNK).astype(BF16)
            at = columns(c, n)
            total = dense[:, at] + dot(pick_hi[...], rows) + dot(pick_lo[...], rows)
            part[c, :, within_half(n)] = total.astype(BF16)
            return carry

        lax.fori_loop(0, HALF // CHUNK, step, 0)
        out = []
        for d in (2, 1, 3):
            peer = lax.rem(tp + d, TP)
            rows_at = pl.ds(pl.multiple_of(peer * OWN, OWN), OWN)
            copy = remote(part.at[c, rows_at], red.at[c, d - 1], red_s.at[a, c, d - 1], red_r.at[a, c, d - 1], (pod, me, peer))
            copy.start()
            out.append(copy)
        return out

    def reduced(a, c, part, red):
        total = part[c, mine, :].astype(F32)
        for d in (1, 2, 3):
            landed = red.at[c, d - 1]
            peer = lax.rem(tp + d, TP)
            remote(landed, landed, red_s.at[a, c, d - 1], red_r.at[a, c, d - 1], (pod, me, peer)).wait_recv()
            total = total + red[c, d - 1].astype(F32)
        return total

    def spread_out(k, ref):
        out = []
        for d in (2, 1, 3):
            peer = lax.rem(tp + d, TP)
            copy = remote(ref, ref, gat_s.at[k, d - 1], gat_r.at[k, d - 1], (pod, me, peer))
            copy.start()
            out.append(copy)
        return out

    def gathered(k, ref, c):
        for d in (1, 2, 3):
            source = lax.rem(tp + 4 - d, TP)
            rows_at = pl.ds(pl.multiple_of(source * OWN, OWN), OWN)
            landed = ref.at[rows_at] if c is None else ref.at[rows_at, pl.ds(c * HALF, HALF)]
            remote(landed, landed, gat_s.at[k, d - 1], gat_r.at[k, d - 1], (pod, me, source)).wait_recv()

    pending = []
    for c in range(2):
        pending += combine(0, c, returned_o, back_o, dense_out, part_o, red_o)
    for c in range(2):
        half = pl.ds(c * HALF, HALF)
        total = reduced(0, c, part_o, red_o)
        layer_out[mine, half] = (tok[mine, half].astype(F32) + total).astype(BF16)
        pending += spread_out(c, layer_out.at[mine, half])
    for c in range(2):
        pending += combine(1, c, returned_g, back_g, dense_grad, part_g, red_g)
    for c in range(2):
        total_g[:, pl.ds(c * HALF, HALF)] = reduced(1, c, part_g, red_g)
    own_in = tok[mine, :].astype(F32)
    own_inverse = lax.rsqrt(jnp.mean(own_in * own_in, axis=1, keepdims=True) + EPS)
    normed = own_in * own_inverse
    scaled = total_g[...] * gain[...]
    project = jnp.mean(scaled * normed, axis=1, keepdims=True)
    grad_in[mine, :] = (
        grad[mine, :].astype(F32) + own_inverse * (scaled - normed * project)
    ).astype(BF16)
    pending += spread_out(2, grad_in.at[mine])
    gathered(0, layer_out, 0)
    gathered(1, layer_out, 1)
    gathered(2, grad_in, None)
    for copies, own in returned_g:
        pending += copies
    for copy in pending + sent_h + sent_g + sent_core + ring_h + ring_g + on_h + on_g:
        copy.wait_send()


def body(tokens, norm_gain, dense_weight, expert_gate_up, expert_down, expert_ids, gate_weights, grad_out):
    vmem = pl.BlockSpec(memory_space=pltpu.VMEM)
    hbm = pl.BlockSpec(memory_space=pl.ANY)
    dma = pltpu.SemaphoreType.DMA
    steps = len(STEPS)
    row_shape = jax.ShapeDtypeStruct((ROWS, D), BF16)
    return pl.pallas_call(
        kernel,
        name="layer",
        out_shape=[row_shape, row_shape],
        in_specs=[vmem, vmem, hbm, hbm, hbm, vmem, vmem, vmem],
        out_specs=[vmem, vmem],
        scratch_shapes=[
            pltpu.VMEM((3, D, FF), BF16),
            pltpu.VMEM((2, D, FF), BF16),
            pltpu.VMEM((D, FF), BF16),
            pltpu.VMEM((ROWS, D), BF16),
            pltpu.VMEM((EP, MOST, QUARTER), BF16),
            pltpu.VMEM((EP, MOST, QUARTER), BF16),
            pltpu.VMEM((TP, EP, MOST, QUARTER), BF16),
            pltpu.VMEM((TP, EP, MOST, QUARTER), BF16),
            pltpu.VMEM((SLOTS, QUARTER), BF16),
            pltpu.VMEM((SLOTS, FF), F32),
            pltpu.VMEM((SLOTS, FF), F32),
            pltpu.VMEM((SLOTS, FF), F32),
            pltpu.VMEM((2, SLOTS, FF), BF16),
            pltpu.VMEM((ROWS, D), F32),
            pltpu.VMEM((ROWS, D), F32),
            pltpu.VMEM((2, EP, MOST, HALF), BF16),
            pltpu.VMEM((2, EP, MOST, HALF), BF16),
            pltpu.VMEM((2, EP, MOST, HALF), BF16),
            pltpu.VMEM((2, EP, MOST, HALF), BF16),
            pltpu.VMEM((2, ROWS, HALF), BF16),
            pltpu.VMEM((2, ROWS, HALF), BF16),
            pltpu.VMEM((2, 3, OWN, HALF), BF16),
            pltpu.VMEM((2, 3, OWN, HALF), BF16),
            pltpu.VMEM((OWN, D), F32),
            pltpu.VMEM((ROWS, SLOTS), BF16),
            pltpu.VMEM((ROWS, SLOTS), BF16),
            dma((5,)),
            dma((3,)),
            dma((3,)),
            dma((2, steps)),
            dma((2, steps)),
            dma((2, 2, 4)),
            dma((2, 2, 4)),
            dma((2, 2, 2)),
            dma((2, 2, 2)),
            dma((6,)),
            dma((2, 2, steps)),
            dma((2, 2, steps)),
            dma((2, 2, 3)),
            dma((2, 2, 3)),
            dma((3, 3)),
            dma((3, 3)),
        ],
        compiler_params=pltpu.CompilerParams(
            collective_id=0, has_side_effects=True, vmem_limit_bytes=63 * 2**20
        ),
    )(
        tokens, norm_gain.reshape(1, D), dense_weight, expert_gate_up, expert_down,
        expert_ids, gate_weights, grad_out,
    )


def solution(mesh):
    rows = P(("outer", "ep"), None)
    in_specs = (rows, P(), P(None, "outer", "tp"), P("ep", None, None, "tp"), P("ep", None, "tp"), rows, rows, rows)
    return jax.shard_map(body, mesh=mesh, in_specs=in_specs, out_specs=(rows, rows), check_vma=False)
```

time: 444 us -> 135 us (0.30); the launches traced: 437 us -> 134 us
  waiting for transfers between devices: 268 us -> 0 us
  Pallas kernels: 0 us -> 125 us
  matrix products: 43 us -> 0 us
  other arithmetic: 42.2 us -> 0 us
  local copies, waits for them, and re-layouts: 45.6 us -> 8.47 us
  starting transfers between devices: 23.6 us -> 0 us
  between operations: 14.8 us -> 0.64 us
    all_to_all x4 -> x0, waiting for transfers between devices: 174 us -> none  [the longest x2 96.4 us: send_rows(): lax.all_to_all(joined, ('outer', 'ep'), split_axis=0, concat_axis=0, tile...]
    pallas_call x0 -> x1, Pallas kernels: none -> 125 us  [body(): pl.pallas_call(kernel, name='layer', out_shape=[row_shape, row_shape], in...]
    psum x2 -> x0, waiting for transfers between devices: 93.5 us -> none  [the longest x1 47.7 us: body(): normed_grad = lax.psum(dense_grad_in + moe_grad, 'tp')]
    dot_general x12 -> x0, matrix products: 43 us -> none  [the longest x6 21.6 us: transpose_dot(): lax.dot_general(left_side, right_side, (((1,), (1,)), ((), ())), preferre...]
    all_to_all x4 -> x0, starting transfers between devices: 23.5 us -> none  [the longest x2 13.5 us: send_rows(): lax.all_to_all(joined, ('outer', 'ep'), split_axis=0, concat_axis=0, tile...]
    reduce_sum x4 -> x0, other arithmetic: 16.3 us -> none  [the longest x1 12.7 us: answer(): return jnp.sum(picked * gate_weights[:, :, None], axis=1)]
    gather x6 -> x0, local copies, waits for them, and re-layouts: 15.2 us -> none  [the longest x4 9.13 us: gather_rows(): jnp.take(padded, row_table, axis=0)]
    select_n x8 -> x0, other arithmetic: 11.3 us -> none  [the longest x3 7.92 us: pod_blocks(): stacked = jnp.where(own_block, local_rows[None], filled[None])]
  transfers between devices with their start and end apart: 7 -> 0, of which waited for: 6 -> 0; matrix products, arithmetic and copies ran while one was open for 14% -> 0% of each run, Pallas kernels for 0% -> 0%
where the time goes in v1:
time: 135 us; the launch traced here: 134 us
  Pallas kernels  125 us (93%)
  local copies, waits for them, and re-layouts  8.47 us (6%)
    pallas_call x1, Pallas kernels, body(): pl.pallas_call(kernel, name='layer', out_shape=[row_shape, row_shape], in...  125 us
    unnamed x4, local copies, waits for them, and re-layouts  7.15 us

profile of v1, /device:TPU:0, one launch (start us, length us, event | category | flops | bytes accessed | tf_op | source)
XLA Modules:
  0.0 134.2 jit_solution(4943170748061103240)
XLA Ops:
  0.6 1.3 reshape.7.gain
  2.0 1.4 %copy.10.ids = s32[128,2]{1,0:T(8,128)} copy(s32[128,2]{0,1:T(2,128)} %param.13) | data formatting | bytes 2048 | tf_op args[5]
  3.4 1.4 %copy.11.weights = f32[128,2]{1,0:T(8,128)} copy(f32[128,2]{0,1:T(2,128)} %param.14) | data formatting | bytes 2048 | tf_op args[6]
  4.8 125.1 %layer.1 = (bf16[128,3584]{1,0:T(8,128)(2,1)}, bf16[128,3584]{1,0:T(8,128)(2,1)}) custom-call(bf16[128,3584]{1,0:T(8,128)(2,1)} %tok.1, f32[1,3584]{1,0:T(1,128)} %reshape.7.gain, bf16[3,1792,640]{2,1,0:T(8,128)(2,1)} %dense_hbm.1, bf16[1,2,3584,640]{3,2,1,0:T(8,128)(2,1)} %gate_up_hbm.1, bf16[1,3584,640]{2,1,0:T(8,128)(2,1)} %down_hbm.1, ...), custom_call_target="tpu_custom_call" | custom-call | tf_op jit(solution)/shard_map/layer/pallas_call | solution.py:386
  129.9 2.2 %copy.14 = bf16[128,3584]{1,0:T(8,128)(2,1)} copy(bf16[128,3584]{1,0:T(8,128)(2,1)} %get-tuple-element.4) | data formatting | bytes 1835008
  132.0 2.2 %copy.15 = bf16[128,3584]{1,0:T(8,128)(2,1)} copy(bf16[128,3584]{1,0:T(8,128)(2,1)} %get-tuple-element.5) | data formatting | bytes 1835008

commit v2 on v1

v2 whole, which is shorter than its diff:
```python
import jax
import jax.numpy as jnp
from jax import lax
from jax.experimental import pallas as pl
from jax.experimental.pallas import tpu as pltpu
from jax.sharding import PartitionSpec as P

MESH = pl.DeviceIdType.MESH
F32 = jnp.float32
BF16 = jnp.bfloat16
ROWS = 128
D = 3584
FF = 640
EP = 16
TP = 4
MOST = 24
SLOTS = EP * MOST
QUARTER = D // TP
RING_H = 640
DIRECT = D - TP * RING_H
HALF = D // 2
PARTS = 4
PART = D // PARTS
OWN = ROWS // TP
EPS = 1e-05
STEPS = [(dz, dx) for dz in (0, 1, 3, 2) for dx in range(4) if (dz, dx) != (0, 0)]
GROUPS = (0, 1, 3, 2)


def silu_parts(values):
    sigmoid_v = jax.nn.sigmoid(values)
    return (values * sigmoid_v, sigmoid_v * (1.0 + values * (1.0 - sigmoid_v)))


def dot(left, right):
    return jnp.dot(left, right, preferred_element_type=F32)


def dot_t(left, right):
    return lax.dot_general(left, right, (((1,), (1,)), ((), ())), preferred_element_type=F32)


def kernel(
    tok, gain, dense_hbm, gate_up_hbm, down_hbm, ids, weights, grad,
    layer_out, grad_in,
    dense_w, gate_up, down, hid, send_h, send_d, send_g, rows_h, rows_d, rows_g, mat_x,
    acc_gate, acc_up, acc_grad, act, dense_out, dense_grad,
    piece_o, piece_g, back_o, back_g, part_o, part_g, red_o, red_g, total_g,
    picks, dense_acc,
    load_sem, core_s, core_r, disp_s, disp_r, ring_s, ring_r, fwd_s, fwd_r,
    self_sem, ret_s, ret_r, red_s, red_r, gat_s, gat_r,
):
    pod, me, tp = lax.axis_index("outer"), lax.axis_index("ep"), lax.axis_index("tp")
    z, x = me // 4, lax.rem(me, 4)
    right, left = lax.rem(tp + 1, TP), lax.rem(tp + 3, TP)

    def expert_at(dz, dx):
        return lax.rem(z + dz + 4, 4) * 4 + lax.rem(x + dx + 4, 4)

    barrier = pltpu.get_barrier_semaphore()
    for dz, dx in STEPS:
        pl.semaphore_signal(barrier, inc=1, device_id=(pod, expert_at(dz, dx), tp), device_id_type=MESH)
    for d in (1, 2, 3):
        pl.semaphore_signal(barrier, inc=1, device_id=(pod, me, lax.rem(tp + d, TP)), device_id_type=MESH)
    pl.semaphore_signal(barrier, inc=1, device_id=(1 - pod, me, tp), device_id_type=MESH)

    loads = [
        pltpu.make_async_copy(gate_up_hbm.at[0], gate_up, load_sem.at[0]),
        pltpu.make_async_copy(down_hbm.at[0], down, load_sem.at[1]),
    ]
    own_rows = pl.ds(pl.multiple_of(pod * HALF, HALF), HALF)
    other_rows = pl.ds(pl.multiple_of((1 - pod) * HALF, HALF), HALF)
    dense_loads = [
        pltpu.make_async_copy(dense_hbm.at[i], dense_w.at[i, own_rows], load_sem.at[2 + i])
        for i in range(3)
    ]
    for load in loads + dense_loads:
        load.start()

    float_in = tok[...].astype(F32)
    inverse = lax.rsqrt(jnp.mean(float_in * float_in, axis=1, keepdims=True) + EPS)
    hid[...] = (float_in * inverse * gain[...].reshape(1, D)).astype(BF16)

    experts = lax.broadcasted_iota(jnp.int32, (EP, ROWS), 0)
    first = (ids[0:1, :] == experts).astype(F32)
    second = (ids[1:2, :] == experts).astype(F32)
    named = (first + second).astype(BF16)
    before = (
        lax.broadcasted_iota(jnp.int32, (ROWS, ROWS), 0)
        < lax.broadcasted_iota(jnp.int32, (ROWS, ROWS), 1)
    ).astype(F32).astype(BF16)
    rank = dot(named, before)
    slot = lax.broadcasted_iota(jnp.int32, (SLOTS, EP), 0)
    low = lax.broadcasted_iota(jnp.int32, (SLOTS, EP), 1) * MOST
    spread = ((slot >= low) & (slot < low + MOST)).astype(F32).astype(BF16)
    slot_f = lax.broadcasted_iota(jnp.int32, (SLOTS, ROWS), 0).astype(F32)
    within = slot_f - MOST * jnp.floor((slot_f + 0.5) * (1.0 / MOST))
    named_at = dot(spread, named)
    rank_at = dot(spread, rank.astype(BF16))
    chosen = jnp.where((named_at > 0.5) & (jnp.abs(rank_at - within) < 0.5), 1.0, 0.0)
    gather = chosen.astype(BF16)

    def pick_rows(source, start, width):
        at = pl.ds(pl.multiple_of(start, 128), width)
        return dot(gather, source[:, at]).reshape(EP, MOST, width).astype(BF16)

    send_h[...] = pick_rows(hid, tp * RING_H, RING_H)

    def make_picks():
        weight = first * weights[0:1, :] + second * weights[1:2, :]
        weight_hi = weight.astype(BF16)
        weight_lo = (weight - weight_hi.astype(F32)).astype(BF16)
        picks[0:ROWS, :] = jnp.transpose(chosen * dot(spread, weight_hi)).astype(BF16)
        picks[ROWS:, :] = jnp.transpose(chosen * dot(spread, weight_lo)).astype(BF16)

    def remote(src, dst, send, recv, device):
        return pltpu.make_async_remote_copy(
            src_ref=src, dst_ref=dst, send_sem=send, recv_sem=recv, device_id=device, device_id_type=MESH
        )

    def dispatch(a, send, rows):
        out = []
        for i, (dz, dx) in enumerate(STEPS):
            peer = expert_at(dz, dx)
            out.append(remote(send.at[peer], rows.at[me], disp_s.at[a, i], disp_r.at[a, i], (pod, peer, tp)))
        for copy in out:
            copy.start()
        own = pltpu.make_async_copy(send.at[me], rows.at[me], self_sem.at[a])
        own.start()
        return out, own

    def dispatched(a, rows, i):
        dz, dx = STEPS[i]
        source = expert_at(-dz, -dx)
        landed = rows.at[source]
        remote(landed, landed, disp_s.at[a, i], disp_r.at[a, i], (pod, source, tp)).wait_recv()

    pl.semaphore_wait(barrier, len(STEPS) + 4)
    sent_h, own_h = dispatch(0, send_h, rows_h.at[tp])
    sent_core = [
        remote(dense_hbm.at[i], dense_w.at[i, own_rows], core_s.at[i], core_r.at[i], (1 - pod, me, tp))
        for i in range(3)
    ]
    for copy in sent_core:
        copy.start()
    send_d[...] = pick_rows(hid, TP * RING_H, DIRECT)
    sent_d, own_d = dispatch(2, send_d, rows_d)
    send_g[...] = pick_rows(grad, tp * QUARTER, QUARTER)
    sent_g, own_g = dispatch(1, send_g, rows_g.at[tp])

    def group_of(rows, q, dz):
        at = pl.multiple_of(lax.rem(z - dz + 4, 4) * 4, 4)
        return rows.at[q, pl.ds(at, 4)]

    def ring_out(a, rows, own):
        out = []
        own.wait()
        for n, group in enumerate(GROUPS):
            for i, (dz, dx) in enumerate(STEPS):
                if dz == group:
                    dispatched(a, rows.at[tp], i)
            block = group_of(rows, tp, group)
            for way, peer in ((0, right), (1, left)):
                copy = remote(block, block, ring_s.at[a, way, n], ring_r.at[a, way, n], (pod, me, peer))
                copy.start()
                out.append(copy)
        return out

    def ring_on(a, rows, way):
        source, peer = ((left, right), (right, left))[way]
        out = []
        for n in (2 * way, 2 * way + 1):
            block = group_of(rows, source, GROUPS[n])
            remote(block, block, ring_s.at[a, way, n], ring_r.at[a, way, n], (pod, me, source)).wait_recv()
            copy = remote(block, block, fwd_s.at[a, way, n % 2], fwd_r.at[a, way, n % 2], (pod, me, peer))
            copy.start()
            out.append(copy)
        return out

    def ring_in(a, rows, way):
        source = (left, right)[way]
        for n in (2 - 2 * way, 3 - 2 * way):
            block = group_of(rows, source, GROUPS[n])
            remote(block, block, ring_s.at[a, way, n], ring_r.at[a, way, n], (pod, me, source)).wait_recv()

    def ring_end(a, rows):
        far = lax.rem(tp + 2, TP)
        for n, group in enumerate(GROUPS):
            way = n // 2
            block = group_of(rows, far, group)
            remote(block, block, fwd_s.at[a, way, n % 2], fwd_r.at[a, way, n % 2], (pod, me, far)).wait_recv()

    def pack(rows, width):
        def step(i, carry):
            block = rows[pl.ds(2 * i, 2)]
            mat_x[pl.ds(pl.multiple_of(i * 2 * MOST, 16), 2 * MOST), 0:width] = (
                block.astype(F32).reshape(2 * MOST, width).astype(BF16)
            )
            return carry

        lax.fori_loop(0, EP // 2, step, 0)

    def forward_part(rows, at, width, start):
        pack(rows, width)
        if start:
            acc_gate[...] = dot(mat_x[:, 0:width], gate_up[0, at, :])
            acc_up[...] = dot(mat_x[:, 0:width], gate_up[1, at, :])
        else:
            acc_gate[...] += dot(mat_x[:, 0:width], gate_up[0, at, :])
            acc_up[...] += dot(mat_x[:, 0:width], gate_up[1, at, :])

    def forward_quarter(q, start):
        at = pl.ds(pl.multiple_of(q * RING_H, RING_H), RING_H)
        forward_part(rows_h.at[q], at, RING_H, start)

    def backward_quarter(q, start):
        pack(rows_g.at[q], QUARTER)
        at = pl.ds(pl.multiple_of(q * QUARTER, QUARTER), QUARTER)
        if start:
            acc_grad[...] = dot(mat_x[:, 0:QUARTER], down[at, :])
        else:
            acc_grad[...] += dot(mat_x[:, 0:QUARTER], down[at, :])

    def dense_in(i, which):
        at = (own_rows, other_rows)[which]
        left_side = (hid, hid, grad)[i]
        if which == 0:
            dense_loads[i].wait()
            dense_acc[i] = dot(left_side[:, at], dense_w[i, at, :])
        else:
            dense_acc[i] += dot(left_side[:, at], dense_w[i, at, :])

    def dense_landed(i):
        landed = dense_w.at[i, other_rows]
        remote(dense_hbm.at[i], landed, core_s.at[i], core_r.at[i], (1 - pod, me, tp)).wait_recv()

    for i in range(3):
        dense_in(i, 0)
    ring_h = ring_out(0, rows_h, own_h)
    for load in loads:
        load.wait()
    forward_quarter(tp, True)
    dense_landed(0)
    dense_in(0, 1)
    on_h = ring_on(0, rows_h, 0)
    dense_landed(1)
    dense_in(1, 1)
    on_h += ring_on(0, rows_h, 1)
    ring_in(0, rows_h, 0)
    forward_quarter(left, False)
    ring_in(0, rows_h, 1)
    forward_quarter(right, False)
    own_d.wait()
    for i in range(len(STEPS)):
        dispatched(2, rows_d, i)
    forward_part(rows_d, pl.ds(TP * RING_H, DIRECT), DIRECT, False)
    ring_end(0, rows_h)
    forward_quarter(lax.rem(tp + 2, TP), False)

    silu, slope = silu_parts(acc_gate[...])
    act[0] = (silu * acc_up[...]).astype(BF16)

    def send_back(a, c, piece, back):
        out = []
        for i, (dz, dx) in enumerate(STEPS):
            peer = expert_at(dz, dx)
            out.append(
                remote(piece.at[c, peer], back.at[c, me], ret_s.at[a, c, i], ret_r.at[a, c, i], (pod, peer, tp))
            )
        for copy in out:
            copy.start()
        own = pltpu.make_async_copy(piece.at[c, me], back.at[c, me], self_sem.at[3 + PARTS * a + c])
        own.start()
        return out, own

    returned_o = []
    for c in range(PARTS):
        cols = pl.ds(c * PART, PART)
        piece_o[c] = dot_t(act[0], down[cols, :]).reshape(EP, MOST, PART).astype(BF16)
        returned_o.append(send_back(0, c, piece_o, back_o))
        if c == 0:
            ring_g = ring_out(1, rows_g, own_g)

    dense_landed(2)
    dense_in(2, 1)
    on_g = ring_on(1, rows_g, 0)
    d_silu, d_slope = silu_parts(dense_acc[0])
    d_up, d_back = dense_acc[1], dense_acc[2]
    d_act = (d_silu * d_up).astype(BF16)
    d_grad_gate = (d_back * d_up * d_slope).astype(BF16)
    d_grad_up = (d_back * d_silu).astype(BF16)
    for c in range(2):
        half = pl.ds(c * HALF, HALF)
        dense_out[:, half] = dot_t(d_act, dense_w[2, half, :]).astype(BF16)
    on_g += ring_on(1, rows_g, 1)
    for c in range(2):
        half = pl.ds(c * HALF, HALF)
        total = dot_t(d_grad_gate, dense_w[0, half, :]) + dot_t(d_grad_up, dense_w[1, half, :])
        dense_grad[:, half] = total.astype(BF16)
    make_picks()

    mine = pl.ds(pl.multiple_of(tp * OWN, OWN), OWN)

    def combine(a, c, returned, back, dense, part, red):
        returned[c][1].wait()
        for i, (dz, dx) in enumerate(STEPS):
            source = expert_at(-dz, -dx)
            landed = back.at[c, source]
            remote(landed, landed, ret_s.at[a, c, i], ret_r.at[a, c, i], (pod, source, tp)).wait_recv()

        rows = back[c].astype(F32).reshape(SLOTS, PART).astype(BF16)
        product = dot(picks[...], rows)
        total = dense[:, pl.ds(c * PART, PART)] + product[:ROWS] + product[ROWS:]
        part[c] = total.astype(BF16)
        out = []
        for d in (2, 1, 3):
            peer = lax.rem(tp + d, TP)
            rows_at = pl.ds(pl.multiple_of(peer * OWN, OWN), OWN)
            copy = remote(part.at[c, rows_at], red.at[c, d - 1], red_s.at[a, c, d - 1], red_r.at[a, c, d - 1], (pod, me, peer))
            copy.start()
            out.append(copy)
        return out

    def reduced(a, c, part, red):
        total = part[c, mine, :].astype(F32)
        for d in (1, 2, 3):
            landed = red.at[c, d - 1]
            peer = lax.rem(tp + d, TP)
            remote(landed, landed, red_s.at[a, c, d - 1], red_r.at[a, c, d - 1], (pod, me, peer)).wait_recv()
            total = total + red[c, d - 1].astype(F32)
        return total

    def spread_out(k, ref):
        out = []
        for d in (2, 1, 3):
            peer = lax.rem(tp + d, TP)
            copy = remote(ref, ref, gat_s.at[k, d - 1], gat_r.at[k, d - 1], (pod, me, peer))
            copy.start()
            out.append(copy)
        return out

    def gathered(k, ref, c):
        for d in (1, 2, 3):
            source = lax.rem(tp + 4 - d, TP)
            rows_at = pl.ds(pl.multiple_of(source * OWN, OWN), OWN)
            landed = ref.at[rows_at, pl.ds(c * PART, PART)] if k < PARTS else ref.at[c, rows_at]
            remote(landed, landed, gat_s.at[k, d - 1], gat_r.at[k, d - 1], (pod, me, source)).wait_recv()

    pending = []

    def combine_o(c):
        return combine(0, c, returned_o, back_o, dense_out, part_o, red_o)

    def reduce_o(c):
        cols = pl.ds(c * PART, PART)
        total = reduced(0, c, part_o, red_o)
        layer_out[mine, cols] = (tok[mine, cols].astype(F32) + total).astype(BF16)
        return spread_out(c, layer_out.at[mine, cols])

    backward_quarter(tp, True)
    ring_in(1, rows_g, 0)
    backward_quarter(left, False)
    ring_in(1, rows_g, 1)
    backward_quarter(right, False)
    pending += combine_o(0)
    pending += combine_o(1)
    ring_end(1, rows_g)
    backward_quarter(lax.rem(tp + 2, TP), False)
    silu, slope = silu_parts(acc_gate[...])
    act[0] = (acc_grad[...] * acc_up[...] * slope).astype(BF16)
    act[1] = (acc_grad[...] * silu).astype(BF16)
    returned_g = []
    for c in range(PARTS):
        cols = pl.ds(c * PART, PART)
        piece = dot_t(act[0], gate_up[0, cols, :]) + dot_t(act[1], gate_up[1, cols, :])
        piece_g[c] = piece.reshape(EP, MOST, PART).astype(BF16)
        returned_g.append(send_back(1, c, piece_g, back_g))
        if c == 1:
            pending += reduce_o(0)

    def combine_g(c):
        return combine(1, c, returned_g, back_g, dense_grad, part_g, red_g)

    def reduce_g(c):
        total_g[c, mine] = reduced(1, c, part_g, red_g).astype(BF16)
        return spread_out(PARTS + c, total_g.at[c, mine])

    pending += combine_o(2)
    pending += reduce_o(1)
    pending += combine_o(3)
    pending += reduce_o(2)
    pending += reduce_o(3)
    pending += combine_g(0)
    for c in range(1, PARTS):
        pending += combine_g(c)
        pending += reduce_g(c - 1)
    pending += reduce_g(PARTS - 1)
    project = jnp.zeros((ROWS, 1), F32)
    for c in range(PARTS):
        cols = pl.ds(c * PART, PART)
        gathered(PARTS + c, total_g, c)
        scaled = total_g[c].astype(F32) * gain[cols].reshape(1, PART)
        project += jnp.sum(scaled * (tok[:, cols].astype(F32) * inverse), axis=1, keepdims=True)
    project = project * (1.0 / D)
    for c in range(PARTS):
        cols = pl.ds(c * PART, PART)
        scaled = total_g[c].astype(F32) * gain[cols].reshape(1, PART)
        normed = tok[:, cols].astype(F32) * inverse
        grad_in[:, cols] = (
            grad[:, cols].astype(F32) + inverse * (scaled - normed * project)
        ).astype(BF16)
    for c in range(PARTS):
        gathered(c, layer_out, c)
    for copies, own in returned_o + returned_g:
        pending += copies
    for copy in pending + sent_h + sent_d + sent_g + sent_core + ring_h + ring_g + on_h + on_g:
        copy.wait_send()


def copy_out(first, second, first_out, second_out):
    first_out[...] = first[...]
    second_out[...] = second[...]


def body(tokens, norm_gain, dense_weight, expert_gate_up, expert_down, expert_ids, gate_weights, grad_out):
    vmem = pl.BlockSpec(memory_space=pltpu.VMEM)
    hbm = pl.BlockSpec(memory_space=pl.ANY)
    dma = pltpu.SemaphoreType.DMA
    steps = len(STEPS)
    row_shape = jax.ShapeDtypeStruct((ROWS, D), BF16)
    results = pl.pallas_call(
        kernel,
        name="layer",
        out_shape=[row_shape, row_shape],
        in_specs=[vmem, vmem, hbm, hbm, hbm, vmem, vmem, vmem],
        out_specs=[vmem, vmem],
        scratch_shapes=[
            pltpu.VMEM((3, D, FF), BF16),
            pltpu.VMEM((2, D, FF), BF16),
            pltpu.VMEM((D, FF), BF16),
            pltpu.VMEM((ROWS, D), BF16),
            pltpu.VMEM((EP, MOST, RING_H), BF16),
            pltpu.VMEM((EP, MOST, DIRECT), BF16),
            pltpu.VMEM((EP, MOST, QUARTER), BF16),
            pltpu.VMEM((TP, EP, MOST, RING_H), BF16),
            pltpu.VMEM((EP, MOST, DIRECT), BF16),
            pltpu.VMEM((TP, EP, MOST, QUARTER), BF16),
            pltpu.VMEM((SLOTS, max(DIRECT, QUARTER)), BF16),
            pltpu.VMEM((SLOTS, FF), F32),
            pltpu.VMEM((SLOTS, FF), F32),
            pltpu.VMEM((SLOTS, FF), F32),
            pltpu.VMEM((2, SLOTS, FF), BF16),
            pltpu.VMEM((ROWS, D), BF16),
            pltpu.VMEM((ROWS, D), BF16),
            pltpu.VMEM((PARTS, EP, MOST, PART), BF16),
            pltpu.VMEM((PARTS, EP, MOST, PART), BF16),
            pltpu.VMEM((PARTS, EP, MOST, PART), BF16),
            pltpu.VMEM((PARTS, EP, MOST, PART), BF16),
            pltpu.VMEM((PARTS, ROWS, PART), BF16),
            pltpu.VMEM((PARTS, ROWS, PART), BF16),
            pltpu.VMEM((PARTS, 3, OWN, PART), BF16),
            pltpu.VMEM((PARTS, 3, OWN, PART), BF16),
            pltpu.VMEM((PARTS, ROWS, PART), BF16),
            pltpu.VMEM((2 * ROWS, SLOTS), BF16),
            pltpu.VMEM((3, ROWS, FF), F32),
            dma((5,)),
            dma((3,)),
            dma((3,)),
            dma((3, steps)),
            dma((3, steps)),
            dma((2, 2, 4)),
            dma((2, 2, 4)),
            dma((2, 2, 2)),
            dma((2, 2, 2)),
            dma((3 + 2 * PARTS,)),
            dma((2, PARTS, steps)),
            dma((2, PARTS, steps)),
            dma((2, PARTS, 3)),
            dma((2, PARTS, 3)),
            dma((2 * PARTS, 3)),
            dma((2 * PARTS, 3)),
        ],
        compiler_params=pltpu.CompilerParams(
            collective_id=0, has_side_effects=True, vmem_limit_bytes=63 * 2**20
        ),
    )(
        tokens, norm_gain, dense_weight, expert_gate_up, expert_down,
        expert_ids.T, gate_weights.T, grad_out,
    )
    return pl.pallas_call(
        copy_out,
        name="copy_out",
        out_shape=[row_shape, row_shape],
        in_specs=[vmem, vmem],
        out_specs=[vmem, vmem],
    )(*results)


def solution(mesh):
    rows = P(("outer", "ep"), None)
    in_specs = (rows, P(), P(None, "outer", "tp"), P("ep", None, None, "tp"), P("ep", None, "tp"), rows, rows, rows)
    return jax.shard_map(body, mesh=mesh, in_specs=in_specs, out_specs=(rows, rows), check_vma=False)
```

time: 135 us -> 117 us (0.87)
  Pallas kernels: 125 us -> 116 us
  local copies, waits for them, and re-layouts: 8.47 us -> 0 us
    pallas_call x1, Pallas kernels: 125 us -> 113 us  [body(): pl.pallas_call(kernel, name='layer', out_shape=[row_shape, row_shape], in...]
    unnamed x4 -> x0, local copies, waits for them, and re-layouts: 7.15 us -> none
    pallas_call x0 -> x1, Pallas kernels: none -> 2.74 us  [body(): pl.pallas_call(copy_out, name='copy_out', out_shape=[row_shape, row_shape...]
where the time goes in v2:
time: 117 us
  Pallas kernels  116 us (99%)
    pallas_call x1, Pallas kernels, body(): pl.pallas_call(kernel, name='layer', out_shape=[row_shape, row_shape], in...  113 us
    pallas_call x1, Pallas kernels, body(): pl.pallas_call(copy_out, name='copy_out', out_shape=[row_shape, row_shape...  2.74 us

profile of v2, /device:TPU:0, one launch (start us, length us, event | category | flops | bytes accessed | tf_op | source)
XLA Modules:
  0.0 116.5 jit_solution(1132453716658225481)
XLA Ops:
  0.6 113.2 %layer.1 = (bf16[128,3584]{1,0:T(8,128)(2,1)}, bf16[128,3584]{1,0:T(8,128)(2,1)}) custom-call(bf16[128,3584]{1,0:T(8,128)(2,1)} %tok.1, f32[3584]{0:T(1024)} %gain.1, bf16[3,1792,640]{2,1,0:T(8,128)(2,1)} %dense_hbm.1, bf16[1,2,3584,640]{3,2,1,0:T(8,128)(2,1)} %gate_up_hbm.1, bf16[1,3584,640]{2,1,0:T(8,128)(2,1)} %down_hbm.1, s32[2,128]{1,0:T(2,128)} %bitcast.2, ...), custom_call_target="tpu_custom_call" | custom-call | tf_op jit(solution)/shard_map/layer/pallas_call | solution.py:431
  113.8 2.7 %copy_out.1 = (bf16[128,3584]{1,0:T(8,128)(2,1)}, bf16[128,3584]{1,0:T(8,128)(2,1)}) custom-call(bf16[128,3584]{1,0:T(8,128)(2,1)} %get-tuple-element.4.first, bf16[128,3584]{1,0:T(8,128)(2,1)} %get-tuple-element.5.second), custom_call_target="tpu_custom_call" | custom-call | tf_op jit(solution)/shard_map/copy_out/pallas_call | solution.py:490

commit v3 on v2

v3 whole, which is shorter than its diff:
```python
import jax
import jax.numpy as jnp
from jax import lax
from jax.experimental import pallas as pl
from jax.experimental.pallas import tpu as pltpu
from jax.sharding import PartitionSpec as P

MESH = pl.DeviceIdType.MESH
F32 = jnp.float32
BF16 = jnp.bfloat16
ROWS = 128
D = 3584
FF = 640
EP = 16
TP = 4
MOST = 24
SLOTS = EP * MOST
RING = 640
DIRECT = D - TP * RING
RING_G = 768
DIRECT_G = D - TP * RING_G
HALF = D // 2
PARTS_O = ((0, 896), (896, 896), (1792, 896), (2688, 896))
BLOCK = 256
WHOLE_G = D - TP * BLOCK
PARTS_G = ((0, 1024), (1024, 1024), (2048, WHOLE_G - 2048))
PARTS = 4
OWN = ROWS // TP
EPS = 1e-05
STEPS = [(dz, dx) for dz in (0, 1, 3, 2) for dx in range(4) if (dz, dx) != (0, 0)]
GROUPS = (0, 1, 3, 2)


def silu_parts(values):
    sigmoid_v = jax.nn.sigmoid(values)
    return (values * sigmoid_v, sigmoid_v * (1.0 + values * (1.0 - sigmoid_v)))


def dot(left, right):
    return jnp.dot(left, right, preferred_element_type=F32)


def dot_t(left, right):
    return lax.dot_general(left, right, (((1,), (1,)), ((), ())), preferred_element_type=F32)


def kernel(
    tok, gain, dense_hbm, gate_up_hbm, down_hbm, ids, weights, grad,
    layer_out, total_g,
    dense_w, gate_up, down, hid, send_h, send_g, rows_h, rows_d, rows_g, rows_e, mat_x,
    acc_gate, acc_up, acc_grad, act, dense_out, dense_grad,
    piece_o, piece_g, back_o, back_g, part_o, part_g, red_o, red_g,
    picks, dense_acc, cross_out, cross_in, merged, back_x, dense_in_x,
    load_sem, core_s, core_r, disp_s, ring_s, ring_r, fwd_s, fwd_r, disp_r, direct_r,
    ret_s, ret_r, red_s, red_r, gat_s, gat_r,
    cross_s, cross_r, dense_s, dense_r, retx_s, retx_r,
):
    pod, me, tp = lax.axis_index("outer"), lax.axis_index("ep"), lax.axis_index("tp")
    z, x = me // 4, lax.rem(me, 4)
    right, left = lax.rem(tp + 1, TP), lax.rem(tp + 3, TP)

    def expert_at(dz, dx):
        return lax.rem(z + dz + 4, 4) * 4 + lax.rem(x + dx + 4, 4)

    barrier = pltpu.get_barrier_semaphore()
    for dz, dx in STEPS:
        pl.semaphore_signal(barrier, inc=1, device_id=(pod, expert_at(dz, dx), tp), device_id_type=MESH)
    for d in (1, 2, 3):
        pl.semaphore_signal(barrier, inc=1, device_id=(pod, me, lax.rem(tp + d, TP)), device_id_type=MESH)
    pl.semaphore_signal(barrier, inc=1, device_id=(1 - pod, me, tp), device_id_type=MESH)

    loads = [
        pltpu.make_async_copy(gate_up_hbm.at[0], gate_up, load_sem.at[0]),
        pltpu.make_async_copy(down_hbm.at[0], down, load_sem.at[1]),
    ]
    own_rows = pl.ds(pl.multiple_of(pod * HALF, HALF), HALF)
    other_rows = pl.ds(pl.multiple_of((1 - pod) * HALF, HALF), HALF)
    dense_loads = [
        pltpu.make_async_copy(dense_hbm.at[i], dense_w.at[i, own_rows], load_sem.at[2 + i])
        for i in range(3)
    ]
    for load in loads + dense_loads:
        load.start()

    float_in = tok[...].astype(F32)
    inverse = lax.rsqrt(jnp.mean(float_in * float_in, axis=1, keepdims=True) + EPS)
    hid[...] = (float_in * inverse * gain[...].reshape(1, D)).astype(BF16)

    experts = lax.broadcasted_iota(jnp.int32, (EP, ROWS), 0)
    first = (ids[0:1, :] == experts).astype(F32)
    second = (ids[1:2, :] == experts).astype(F32)
    named = (first + second).astype(BF16)
    before = (
        lax.broadcasted_iota(jnp.int32, (ROWS, ROWS), 0)
        < lax.broadcasted_iota(jnp.int32, (ROWS, ROWS), 1)
    ).astype(F32).astype(BF16)
    rank = dot(named, before)
    slot = lax.broadcasted_iota(jnp.int32, (SLOTS, EP), 0)
    low = lax.broadcasted_iota(jnp.int32, (SLOTS, EP), 1) * MOST
    spread = ((slot >= low) & (slot < low + MOST)).astype(F32).astype(BF16)
    slot_f = lax.broadcasted_iota(jnp.int32, (SLOTS, ROWS), 0).astype(F32)
    within = slot_f - MOST * jnp.floor((slot_f + 0.5) * (1.0 / MOST))
    named_at = dot(spread, named)
    rank_at = dot(spread, rank.astype(BF16))
    chosen = jnp.where((named_at > 0.5) & (jnp.abs(rank_at - within) < 0.5), 1.0, 0.0)
    gather = chosen.astype(BF16)

    def pick_rows(source, start, width):
        at = pl.ds(pl.multiple_of(start, 128), width)
        return dot(gather, source[:, at]).reshape(EP, MOST, width).astype(BF16)

    send_h[...] = pick_rows(hid, tp * RING, RING)

    def make_picks():
        weight = first * weights[0:1, :] + second * weights[1:2, :]
        weight_hi = weight.astype(BF16)
        weight_lo = (weight - weight_hi.astype(F32)).astype(BF16)
        picks[0:ROWS, :] = jnp.transpose(chosen * dot(spread, weight_hi)).astype(BF16)
        picks[ROWS:, :] = jnp.transpose(chosen * dot(spread, weight_lo)).astype(BF16)

    def remote(src, dst, send, recv, device):
        return pltpu.make_async_remote_copy(
            src_ref=src, dst_ref=dst, send_sem=send, recv_sem=recv, device_id=device, device_id_type=MESH
        )

    def arrived(view, sem):
        remote(view, view, sem, sem, (pod, me, right)).wait_recv()

    def sent(view, sem):
        remote(view, view, sem, sem, (pod, me, right)).wait_send()

    def dispatch(a, send, rows, recv):
        for dz, dx in STEPS:
            peer = expert_at(dz, dx)
            remote(send.at[peer], rows.at[me], disp_s.at[a], recv(dz), (pod, peer, tp)).start()
        pltpu.make_async_copy(send.at[me], rows.at[me], recv(0)).start()

    first_cols, first_cols_g = pl.ds(0, DIRECT), pl.ds(0, DIRECT_G)
    piece_o[:, :, first_cols] = pick_rows(hid, TP * RING, DIRECT)
    pl.semaphore_wait(barrier, len(STEPS) + 4)
    dispatch(0, send_h, rows_h.at[tp], lambda dz: disp_r.at[0, dz])
    for i in range(3):
        remote(
            dense_hbm.at[i], dense_w.at[i, own_rows], core_s.at[i], core_r.at[i], (1 - pod, me, tp)
        ).start()
    dispatch(2, piece_o.at[:, :, first_cols], rows_d, lambda dz: direct_r.at[0])
    send_g[...] = pick_rows(grad, tp * RING_G, RING_G)
    dispatch(1, send_g, rows_g.at[tp], lambda dz: disp_r.at[1, dz])
    if DIRECT_G:
        piece_g[:, :, first_cols_g] = pick_rows(grad, TP * RING_G, DIRECT_G)
        dispatch(3, piece_g.at[:, :, first_cols_g], rows_e, lambda dz: direct_r.at[1])

    def group_of(rows, q, dz):
        at = pl.multiple_of(lax.rem(z - dz + 4, 4) * 4, 4)
        return rows.at[q, pl.ds(at, 4)]

    def ring_out(a, rows, some=(0, 1, 2, 3)):
        for n in some:
            block = group_of(rows, tp, GROUPS[n])
            arrived(block, disp_r.at[a, GROUPS[n]])
            for way, peer in ((0, right), (1, left)):
                remote(block, block, ring_s.at[a], ring_r.at[a, way, n], (pod, me, peer)).start()

    def ring_on(a, rows, way):
        source, peer = ((left, right), (right, left))[way]
        for n in (2 * way, 2 * way + 1):
            block = group_of(rows, source, GROUPS[n])
            arrived(block, ring_r.at[a, way, n])
            remote(block, block, fwd_s.at[a], fwd_r.at[a], (pod, me, peer)).start()

    def ring_in(a, rows, way):
        source = (left, right)[way]
        for n in (2 - 2 * way, 3 - 2 * way):
            arrived(group_of(rows, source, GROUPS[n]), ring_r.at[a, way, n])

    def ring_end(a, rows):
        arrived(rows.at[lax.rem(tp + 2, TP)], fwd_r.at[a])

    def pack(rows, width):
        def step(i, carry):
            block = rows[pl.ds(2 * i, 2)]
            mat_x[pl.ds(pl.multiple_of(i * 2 * MOST, 16), 2 * MOST), 0:width] = (
                block.astype(F32).reshape(2 * MOST, width).astype(BF16)
            )
            return carry

        lax.fori_loop(0, EP // 2, step, 0)

    def forward_part(rows, at, width, start):
        pack(rows, width)
        if start:
            acc_gate[...] = dot(mat_x[:, 0:width], gate_up[0, at, :])
            acc_up[...] = dot(mat_x[:, 0:width], gate_up[1, at, :])
        else:
            acc_gate[...] += dot(mat_x[:, 0:width], gate_up[0, at, :])
            acc_up[...] += dot(mat_x[:, 0:width], gate_up[1, at, :])

    def forward_quarter(q, start):
        at = pl.ds(pl.multiple_of(q * RING, RING), RING)
        forward_part(rows_h.at[q], at, RING, start)

    def backward_part(rows, at, width, start):
        pack(rows, width)
        if start:
            acc_grad[...] = dot(mat_x[:, 0:width], down[at, :])
        else:
            acc_grad[...] += dot(mat_x[:, 0:width], down[at, :])

    def backward_quarter(q, start):
        at = pl.ds(pl.multiple_of(q * RING_G, RING_G), RING_G)
        backward_part(rows_g.at[q], at, RING_G, start)

    def dense_in(i, which):
        at = (own_rows, other_rows)[which]
        left_side = (hid, hid, grad)[i]
        if which == 0:
            dense_loads[i].wait()
            dense_acc[i] = dot(left_side[:, at], dense_w[i, at, :])
        else:
            dense_acc[i] += dot(left_side[:, at], dense_w[i, at, :])

    def dense_landed(i):
        landed = dense_w.at[i, other_rows]
        remote(dense_hbm.at[i], landed, core_s.at[i], core_r.at[i], (1 - pod, me, tp)).wait_recv()

    for i in range(3):
        dense_in(i, 0)
    ring_out(0, rows_h)
    for load in loads:
        load.wait()
    forward_quarter(tp, True)
    dense_landed(0)
    dense_in(0, 1)
    ring_on(0, rows_h, 0)
    dense_landed(1)
    dense_in(1, 1)
    ring_on(0, rows_h, 1)
    ring_in(0, rows_h, 0)
    forward_quarter(left, False)
    ring_in(0, rows_h, 1)
    forward_quarter(right, False)
    arrived(rows_d, direct_r.at[0])
    forward_part(rows_d, pl.ds(TP * RING, DIRECT), DIRECT, False)
    ring_out(1, rows_g, (0, 1))
    ring_end(0, rows_h)
    forward_quarter(lax.rem(tp + 2, TP), False)
    ring_out(1, rows_g, (2, 3))
    peers = pl.ds(0, len(STEPS))
    sent(piece_o.at[peers, :, first_cols], disp_s.at[2])

    silu, slope = silu_parts(acc_gate[...])
    act[0] = (silu * acc_up[...]).astype(BF16)

    def block_at(q):
        return pl.ds(pl.multiple_of(WHOLE_G + q * BLOCK, BLOCK), BLOCK)

    def span(a, c):
        return pl.ds(*((PARTS_O, PARTS_G)[a][c]))

    def send_back(a, c, piece, back):
        cols = span(a, c)
        for dz, dx in STEPS:
            peer = expert_at(dz, dx)
            remote(
                piece.at[peer, :, cols], back.at[me, :, cols], ret_s.at[a, c], ret_r.at[a, c], (pod, peer, tp)
            ).start()
        pltpu.make_async_copy(piece.at[me, :, cols], back.at[me, :, cols], ret_r.at[a, c]).start()

    for c in range(PARTS):
        cols = span(0, c)
        piece_o[:, :, cols] = dot_t(act[0], down[cols, :]).reshape(EP, MOST, cols.size).astype(BF16)
        send_back(0, c, piece_o, back_o)

    dense_landed(2)
    dense_in(2, 1)
    ring_on(1, rows_g, 0)
    d_silu, d_slope = silu_parts(dense_acc[0])
    d_up, d_back = dense_acc[1], dense_acc[2]
    d_act = (d_silu * d_up).astype(BF16)
    d_grad_gate = (d_back * d_up * d_slope).astype(BF16)
    d_grad_up = (d_back * d_silu).astype(BF16)
    for c in range(2):
        half = pl.ds(c * HALF, HALF)
        dense_out[:, half] = dot_t(d_act, dense_w[2, half, :]).astype(BF16)
    ring_on(1, rows_g, 1)
    for c in range(2):
        half = pl.ds(c * HALF, HALF)
        total = dot_t(d_grad_gate, dense_w[0, half, :]) + dot_t(d_grad_up, dense_w[1, half, :])
        dense_grad[:, half] = total.astype(BF16)
    make_picks()
    for d in (2, 1, 3):
        peer = lax.rem(tp + d, TP)
        remote(
            dense_grad.at[:, block_at(peer)], dense_in_x.at[d - 1], dense_s.at[0], dense_r.at[0], (pod, me, peer)
        ).start()
    mine = pl.ds(pl.multiple_of(tp * OWN, OWN), OWN)

    def combine(a, c, back, dense, part, red):
        cols = span(a, c)
        arrived(back.at[:, :, cols], ret_r.at[a, c])
        rows = back[:, :, cols].astype(F32).reshape(SLOTS, cols.size).astype(BF16)
        product = dot(picks[...], rows)
        total = dense[:, cols].astype(F32) + product[:ROWS] + product[ROWS:]
        part[:, cols] = total.astype(BF16)
        for d in (2, 1, 3):
            peer = lax.rem(tp + d, TP)
            rows_at = pl.ds(pl.multiple_of(peer * OWN, OWN), OWN)
            remote(
                part.at[rows_at, cols], red.at[d - 1, :, cols], red_s.at[a, c], red_r.at[a, c], (pod, me, peer)
            ).start()

    def reduced(a, c, part, red):
        cols = span(a, c)
        total = part[mine, cols].astype(F32)
        arrived(red.at[:, :, cols], red_r.at[a, c])
        for d in range(3):
            total = total + red[d, :, cols].astype(F32)
        return total

    def spread_out(k, ref):
        for d in (2, 1, 3):
            remote(ref, ref, gat_s.at[k], gat_r.at[k], (pod, me, lax.rem(tp + d, TP))).start()

    others = pl.ds(0, ROWS - OWN)

    def combine_o(c):
        combine(0, c, back_o, dense_out, part_o, red_o)

    def reduce_o(c):
        cols = span(0, c)
        total = reduced(0, c, part_o, red_o)
        layer_out[mine, cols] = (tok[mine, cols].astype(F32) + total).astype(BF16)
        spread_out(c, layer_out.at[mine, cols])

    backward_quarter(tp, True)
    ring_in(1, rows_g, 0)
    backward_quarter(left, False)
    ring_in(1, rows_g, 1)
    backward_quarter(right, False)
    if DIRECT_G:
        arrived(rows_e, direct_r.at[1])
        backward_part(rows_e, pl.ds(TP * RING_G, DIRECT_G), DIRECT_G, False)
    combine_o(0)
    ring_end(1, rows_g)
    backward_quarter(lax.rem(tp + 2, TP), False)
    if DIRECT_G:
        sent(piece_g.at[peers, :, first_cols_g], disp_s.at[3])
    silu, slope = silu_parts(acc_gate[...])
    act[0] = (acc_grad[...] * acc_up[...] * slope).astype(BF16)
    act[1] = (acc_grad[...] * silu).astype(BF16)

    def grad_piece(cols):
        return dot_t(act[0], gate_up[0, cols, :]) + dot_t(act[1], gate_up[1, cols, :])

    for d in (2, 1, 3):
        peer = lax.rem(tp + d, TP)
        cross_out[d - 1] = grad_piece(block_at(peer)).reshape(EP, MOST, BLOCK).astype(BF16)
        remote(
            cross_out.at[d - 1], cross_in.at[d - 1], cross_s.at[0], cross_r.at[0], (pod, me, peer)
        ).start()
    for c in range(len(PARTS_G)):
        cols = span(1, c)
        piece_g[:, :, cols] = grad_piece(cols).reshape(EP, MOST, cols.size).astype(BF16)
        send_back(1, c, piece_g, back_g)
        if c == 0:
            combine_o(1)
            reduce_o(0)
    merged[...] = grad_piece(block_at(tp)).reshape(EP, MOST, BLOCK).astype(BF16)

    def merge():
        total = merged[...].astype(F32)
        arrived(cross_in, cross_r.at[0])
        for d in range(3):
            total = total + cross_in[d].astype(F32)
        merged[...] = total.astype(BF16)
        for dz, dx in STEPS:
            peer = expert_at(dz, dx)
            remote(merged.at[peer], back_x.at[me], retx_s.at[0], retx_r.at[0], (pod, peer, tp)).start()
        pltpu.make_async_copy(merged.at[me], back_x.at[me], retx_r.at[0]).start()

    def combine_x():
        arrived(back_x, retx_r.at[0])
        rows = back_x[...].astype(F32).reshape(SLOTS, BLOCK).astype(BF16)
        product = dot(picks[...], rows)
        total = dense_grad[:, block_at(tp)].astype(F32) + product[:ROWS] + product[ROWS:]
        arrived(dense_in_x, dense_r.at[0])
        for d in range(3):
            total = total + dense_in_x[d].astype(F32)
        total_g[:, block_at(tp)] = total.astype(BF16)
        spread_out(2 * PARTS - 1, total_g.at[:, block_at(tp)])

    def combine_g(c):
        combine(1, c, back_g, dense_grad, part_g, red_g)

    def reduce_g(c):
        cols = span(1, c)
        total_g[mine, cols] = reduced(1, c, part_g, red_g).astype(BF16)
        spread_out(PARTS + c, total_g.at[mine, cols])

    combine_o(2)
    reduce_o(1)
    combine_o(3)
    merge()
    reduce_o(2)
    reduce_o(3)
    combine_g(0)
    for c in range(1, len(PARTS_G)):
        combine_g(c)
        reduce_g(c - 1)
    combine_x()
    reduce_g(len(PARTS_G) - 1)

    for c in range(PARTS):
        view = layer_out.at[others, span(0, c)]
        arrived(view, gat_r.at[c])
        sent(view, gat_s.at[c])
        sent(red_o.at[:, :, span(0, c)], red_s.at[0, c])
        sent(piece_o.at[peers, :, span(0, c)], ret_s.at[0, c])
    for c in range(len(PARTS_G)):
        view = total_g.at[others, span(1, c)]
        arrived(view, gat_r.at[PARTS + c])
        sent(view, gat_s.at[PARTS + c])
        sent(red_g.at[:, :, span(1, c)], red_s.at[1, c])
        sent(piece_g.at[peers, :, span(1, c)], ret_s.at[1, c])
    arrived(dense_in_x, gat_r.at[2 * PARTS - 1])
    sent(dense_in_x, gat_s.at[2 * PARTS - 1])
    sent(dense_in_x, dense_s.at[0])
    sent(cross_out, cross_s.at[0])
    sent(merged.at[peers], retx_s.at[0])
    for i in range(3):
        sent(dense_hbm.at[i], core_s.at[i])
    for a, send, rows in ((0, send_h, rows_h), (1, send_g, rows_g)):
        sent(send.at[peers], disp_s.at[a])
        sent(rows.at[pl.ds(0, 2)], ring_s.at[a])
        sent(rows.at[0], fwd_s.at[a])


def finish(tok, gain, grad, total_g, layer_in, layer_out, grad_in):
    layer_out[...] = layer_in[...]
    float_in = tok[...].astype(F32)
    inverse = lax.rsqrt(jnp.mean(float_in * float_in, axis=1, keepdims=True) + EPS)
    normed = float_in * inverse
    scaled = total_g[...].astype(F32) * gain[...].reshape(1, D)
    project = jnp.mean(scaled * normed, axis=1, keepdims=True)
    grad_in[...] = (grad[...].astype(F32) + inverse * (scaled - normed * project)).astype(BF16)


def body(tokens, norm_gain, dense_weight, expert_gate_up, expert_down, expert_ids, gate_weights, grad_out):
    vmem = pl.BlockSpec(memory_space=pltpu.VMEM)
    hbm = pl.BlockSpec(memory_space=pl.ANY)
    dma = pltpu.SemaphoreType.DMA
    steps = len(STEPS)
    row_shape = jax.ShapeDtypeStruct((ROWS, D), BF16)
    layer_sum, grad_sum = pl.pallas_call(
        kernel,
        name="layer",
        out_shape=[row_shape, row_shape],
        in_specs=[vmem, vmem, hbm, hbm, hbm, vmem, vmem, vmem],
        out_specs=[vmem, vmem],
        scratch_shapes=[
            pltpu.VMEM((3, D, FF), BF16),
            pltpu.VMEM((2, D, FF), BF16),
            pltpu.VMEM((D, FF), BF16),
            pltpu.VMEM((ROWS, D), BF16),
            pltpu.VMEM((EP, MOST, RING), BF16),
            pltpu.VMEM((EP, MOST, RING_G), BF16),
            pltpu.VMEM((TP, EP, MOST, RING), BF16),
            pltpu.VMEM((EP, MOST, DIRECT), BF16),
            pltpu.VMEM((TP, EP, MOST, RING_G), BF16),
            pltpu.VMEM((EP, MOST, max(DIRECT_G, 128)), BF16),
            pltpu.VMEM((SLOTS, max(DIRECT, RING_G)), BF16),
            pltpu.VMEM((SLOTS, FF), F32),
            pltpu.VMEM((SLOTS, FF), F32),
            pltpu.VMEM((SLOTS, FF), F32),
            pltpu.VMEM((2, SLOTS, FF), BF16),
            pltpu.VMEM((ROWS, D), BF16),
            pltpu.VMEM((ROWS, D), BF16),
            pltpu.VMEM((EP, MOST, D), BF16),
            pltpu.VMEM((EP, MOST, WHOLE_G), BF16),
            pltpu.VMEM((EP, MOST, D), BF16),
            pltpu.VMEM((EP, MOST, WHOLE_G), BF16),
            pltpu.VMEM((ROWS, D), BF16),
            pltpu.VMEM((ROWS, WHOLE_G), BF16),
            pltpu.VMEM((3, OWN, D), BF16),
            pltpu.VMEM((3, OWN, WHOLE_G), BF16),
            pltpu.VMEM((2 * ROWS, SLOTS), BF16),
            pltpu.VMEM((3, ROWS, FF), F32),
            pltpu.VMEM((3, EP, MOST, BLOCK), BF16),
            pltpu.VMEM((3, EP, MOST, BLOCK), BF16),
            pltpu.VMEM((EP, MOST, BLOCK), BF16),
            pltpu.VMEM((EP, MOST, BLOCK), BF16),
            pltpu.VMEM((3, ROWS, BLOCK), BF16),
            dma((5,)),
            dma((3,)),
            dma((3,)),
            dma((4,)),
            dma((2,)),
            dma((2, 2, 4)),
            dma((2,)),
            dma((2,)),
            dma((2, 4)),
            dma((2,)),
            dma((2, PARTS)),
            dma((2, PARTS)),
            dma((2, PARTS)),
            dma((2, PARTS)),
            dma((2 * PARTS,)),
            dma((2 * PARTS,)),
            dma((1,)),
            dma((1,)),
            dma((1,)),
            dma((1,)),
            dma((1,)),
            dma((1,)),
        ],
        compiler_params=pltpu.CompilerParams(
            collective_id=0, has_side_effects=True, vmem_limit_bytes=63 * 2**20
        ),
    )(
        tokens, norm_gain, dense_weight, expert_gate_up, expert_down,
        expert_ids.T, gate_weights.T, grad_out,
    )
    block = pl.BlockSpec((ROWS // 2, D), lambda i: (i, 0))
    return pl.pallas_call(
        finish,
        name="finish",
        grid=(2,),
        out_shape=[row_shape, row_shape],
        in_specs=[block, pl.BlockSpec((D,), lambda i: (0,)), block, block, block],
        out_specs=[block, block],
    )(tokens, norm_gain, grad_out, grad_sum, layer_sum)


def solution(mesh):
    rows = P(("outer", "ep"), None)
    in_specs = (rows, P(), P(None, "outer", "tp"), P("ep", None, None, "tp"), P("ep", None, "tp"), rows, rows, rows)
    return jax.shard_map(body, mesh=mesh, in_specs=in_specs, out_specs=(rows, rows), check_vma=False)
```

time: 117 us -> 107 us (0.915)
  Pallas kernels: 116 us -> 106 us
    pallas_call x1, Pallas kernels: 113 us -> 102 us  [body(): pl.pallas_call(kernel, name='layer', out_shape=[row_shape, row_shape], in...]
where the time goes in v3:
time: 107 us
  Pallas kernels  106 us (99%)
    pallas_call x1, Pallas kernels, body(): pl.pallas_call(kernel, name='layer', out_shape=[row_shape, row_shape], in...  102 us
    pallas_call x1, Pallas kernels, body(): pl.pallas_call(finish, name='finish', grid=(2,), out_shape=[row_shape, ro...  3.65 us

profile of v3, /device:TPU:0, one launch (start us, length us, event | category | flops | bytes accessed | tf_op | source)
XLA Modules:
  0.0 106.7 jit_solution(16328215765691574822)
XLA Ops:
  0.6 102.4 %layer.1 = (bf16[128,3584]{1,0:T(8,128)(2,1)}, bf16[128,3584]{1,0:T(8,128)(2,1)}) custom-call(bf16[128,3584]{1,0:T(8,128)(2,1)} %tok.3, f32[3584]{0:T(1024)} %gain.3, bf16[3,1792,640]{2,1,0:T(8,128)(2,1)} %dense_hbm.1, bf16[1,2,3584,640]{3,2,1,0:T(8,128)(2,1)} %gate_up_hbm.1, bf16[1,3584,640]{2,1,0:T(8,128)(2,1)} %down_hbm.1, s32[2,128]{1,0:T(2,128)} %bitcast.2, ...), custom_call_target="tpu_custom_call" | custom-call | tf_op jit(solution)/shard_map/layer/pallas_call | solution.py:454
  103.0 3.7 %finish.1 = (bf16[128,3584]{1,0:T(8,128)(2,1)}, bf16[128,3584]{1,0:T(8,128)(2,1)}) custom-call(bf16[128,3584]{1,0:T(8,128)(2,1)} %tok.3, f32[3584]{0:T(1024)} %gain.3, bf16[128,3584]{1,0:T(8,128)(2,1)} %grad.3, bf16[128,3584]{1,0:T(8,128)(2,1)} %get-tuple-element.4.total_g, bf16[128,3584]{1,0:T(8,128)(2,1)} %get-tuple-element.5.layer_in), custom_call_target="tpu_custom_call" | custom-call | tf_op jit(solution)/shard_map/finish/pallas_call | solution.py:524

commit v4 on v3

--- a/solution.py
+++ b/solution.py
@@ -23,8 +23,8 @@
 PARTS_O = ((0, 896), (896, 896), (1792, 896), (2688, 896))
 BLOCK = 256
 WHOLE_G = D - TP * BLOCK
-PARTS_G = ((0, 1024), (1024, 1024), (2048, WHOLE_G - 2048))
-PARTS = 4
+PARTS_G = ((0, 768), (768, 768), (1536, 640), (2176, WHOLE_G - 2176))
+PARTS = 5
 OWN = ROWS // TP
 EPS = 1e-05
 STEPS = [(dz, dx) for dz in (0, 1, 3, 2) for dx in range(4) if (dz, dx) != (0, 0)]
@@ -45,9 +45,9 @@
 
 
 def kernel(
-    tok, gain, dense_hbm, gate_up_hbm, down_hbm, ids, weights, grad,
+    tok_hbm, gain, dense_hbm, gate_up_hbm, down_hbm, ids, weights, grad_hbm,
     layer_out, total_g,
-    dense_w, gate_up, down, hid, send_h, send_g, rows_h, rows_d, rows_g, rows_e, mat_x,
+    tok, grad, dense_w, gate_up, down, hid, send_h, send_g, rows_h, rows_d, rows_g, rows_e, mat_x,
     acc_gate, acc_up, acc_grad, act, dense_out, dense_grad,
     piece_o, piece_g, back_o, back_g, part_o, part_g, red_o, red_g,
     picks, dense_acc, cross_out, cross_in, merged, back_x, dense_in_x,
@@ -69,6 +69,10 @@
         pl.semaphore_signal(barrier, inc=1, device_id=(pod, me, lax.rem(tp + d, TP)), device_id_type=MESH)
     pl.semaphore_signal(barrier, inc=1, device_id=(1 - pod, me, tp), device_id_type=MESH)
 
+    row_loads = [
+        pltpu.make_async_copy(tok_hbm, tok, load_sem.at[5]),
+        pltpu.make_async_copy(grad_hbm, grad, load_sem.at[6]),
+    ]
     loads = [
         pltpu.make_async_copy(gate_up_hbm.at[0], gate_up, load_sem.at[0]),
         pltpu.make_async_copy(down_hbm.at[0], down, load_sem.at[1]),
@@ -79,8 +83,9 @@
         pltpu.make_async_copy(dense_hbm.at[i], dense_w.at[i, own_rows], load_sem.at[2 + i])
         for i in range(3)
     ]
-    for load in loads + dense_loads:
+    for load in row_loads + loads + dense_loads:
         load.start()
+    row_loads[0].wait()
 
     float_in = tok[...].astype(F32)
     inverse = lax.rsqrt(jnp.mean(float_in * float_in, axis=1, keepdims=True) + EPS)
@@ -144,6 +149,7 @@
             dense_hbm.at[i], dense_w.at[i, own_rows], core_s.at[i], core_r.at[i], (1 - pod, me, tp)
         ).start()
     dispatch(2, piece_o.at[:, :, first_cols], rows_d, lambda dz: direct_r.at[0])
+    row_loads[1].wait()
     send_g[...] = pick_rows(grad, tp * RING_G, RING_G)
     dispatch(1, send_g, rows_g.at[tp], lambda dz: disp_r.at[1, dz])
     if DIRECT_G:
@@ -266,7 +272,7 @@
             ).start()
         pltpu.make_async_copy(piece.at[me, :, cols], back.at[me, :, cols], ret_r.at[a, c]).start()
 
-    for c in range(PARTS):
+    for c in range(4):
         cols = span(0, c)
         piece_o[:, :, cols] = dot_t(act[0], down[cols, :]).reshape(EP, MOST, cols.size).astype(BF16)
         send_back(0, c, piece_o, back_o)
@@ -317,9 +323,10 @@
             total = total + red[d, :, cols].astype(F32)
         return total
 
-    def spread_out(k, ref):
+    def spread_out(k, ref, target):
         for d in (2, 1, 3):
-            remote(ref, ref, gat_s.at[k], gat_r.at[k], (pod, me, lax.rem(tp + d, TP))).start()
+            remote(ref, target, gat_s.at[k], gat_r.at[k], (pod, me, lax.rem(tp + d, TP))).start()
+        pltpu.make_async_copy(ref, target, gat_r.at[k]).start()
 
     others = pl.ds(0, ROWS - OWN)
 
@@ -329,8 +336,8 @@
     def reduce_o(c):
         cols = span(0, c)
         total = reduced(0, c, part_o, red_o)
-        layer_out[mine, cols] = (tok[mine, cols].astype(F32) + total).astype(BF16)
-        spread_out(c, layer_out.at[mine, cols])
+        part_o[mine, cols] = (tok[mine, cols].astype(F32) + total).astype(BF16)
+        spread_out(c, part_o.at[mine, cols], layer_out.at[mine, cols])
 
     backward_quarter(tp, True)
     ring_in(1, rows_g, 0)
@@ -386,16 +393,16 @@
         arrived(dense_in_x, dense_r.at[0])
         for d in range(3):
             total = total + dense_in_x[d].astype(F32)
-        total_g[:, block_at(tp)] = total.astype(BF16)
-        spread_out(2 * PARTS - 1, total_g.at[:, block_at(tp)])
+        dense_in_x[0] = total.astype(BF16)
+        spread_out(2 * PARTS - 1, dense_in_x.at[0], total_g.at[:, block_at(tp)])
 
     def combine_g(c):
         combine(1, c, back_g, dense_grad, part_g, red_g)
 
     def reduce_g(c):
         cols = span(1, c)
-        total_g[mine, cols] = reduced(1, c, part_g, red_g).astype(BF16)
-        spread_out(PARTS + c, total_g.at[mine, cols])
+        part_g[mine, cols] = reduced(1, c, part_g, red_g).astype(BF16)
+        spread_out(PARTS + c, part_g.at[mine, cols], total_g.at[mine, cols])
 
     combine_o(2)
     reduce_o(1)
@@ -410,19 +417,17 @@
     combine_x()
     reduce_g(len(PARTS_G) - 1)
 
-    for c in range(PARTS):
-        view = layer_out.at[others, span(0, c)]
-        arrived(view, gat_r.at[c])
-        sent(view, gat_s.at[c])
+    for c in range(4):
+        arrived(layer_out.at[:, span(0, c)], gat_r.at[c])
+        sent(part_o.at[others, span(0, c)], gat_s.at[c])
         sent(red_o.at[:, :, span(0, c)], red_s.at[0, c])
         sent(piece_o.at[peers, :, span(0, c)], ret_s.at[0, c])
     for c in range(len(PARTS_G)):
-        view = total_g.at[others, span(1, c)]
-        arrived(view, gat_r.at[PARTS + c])
-        sent(view, gat_s.at[PARTS + c])
+        arrived(total_g.at[:, span(1, c)], gat_r.at[PARTS + c])
+        sent(part_g.at[others, span(1, c)], gat_s.at[PARTS + c])
         sent(red_g.at[:, :, span(1, c)], red_s.at[1, c])
         sent(piece_g.at[peers, :, span(1, c)], ret_s.at[1, c])
-    arrived(dense_in_x, gat_r.at[2 * PARTS - 1])
+    arrived(total_g.at[:, pl.ds(WHOLE_G, TP * BLOCK)], gat_r.at[2 * PARTS - 1])
     sent(dense_in_x, gat_s.at[2 * PARTS - 1])
     sent(dense_in_x, dense_s.at[0])
     sent(cross_out, cross_s.at[0])
@@ -455,9 +460,11 @@
         kernel,
         name="layer",
         out_shape=[row_shape, row_shape],
-        in_specs=[vmem, vmem, hbm, hbm, hbm, vmem, vmem, vmem],
-        out_specs=[vmem, vmem],
+        in_specs=[hbm, vmem, hbm, hbm, hbm, vmem, vmem, hbm],
+        out_specs=[hbm, hbm],
         scratch_shapes=[
+            pltpu.VMEM((ROWS, D), BF16),
+            pltpu.VMEM((ROWS, D), BF16),
             pltpu.VMEM((3, D, FF), BF16),
             pltpu.VMEM((2, D, FF), BF16),
             pltpu.VMEM((D, FF), BF16),
@@ -490,7 +497,7 @@
             pltpu.VMEM((EP, MOST, BLOCK), BF16),
             pltpu.VMEM((EP, MOST, BLOCK), BF16),
             pltpu.VMEM((3, ROWS, BLOCK), BF16),
-            dma((5,)),
+            dma((7,)),
             dma((3,)),
             dma((3,)),
             dma((4,)),

time: 107 us -> 104 us (0.972)
  Pallas kernels: 106 us -> 103 us
    pallas_call x1, Pallas kernels: 102 us -> 99.7 us  [body(): pl.pallas_call(kernel, name='layer', out_shape=[row_shape, row_shape], in...]
where the time goes in v4:
time: 104 us
  Pallas kernels  103 us (99%)
    pallas_call x1, Pallas kernels, body(): pl.pallas_call(kernel, name='layer', out_shape=[row_shape, row_shape], in...  99.7 us
    pallas_call x1, Pallas kernels, body(): pl.pallas_call(finish, name='finish', grid=(2,), out_shape=[row_shape, ro...  3.65 us

profile of v4, /device:TPU:0, one launch (start us, length us, event | category | flops | bytes accessed | tf_op | source)
XLA Modules:
  0.0 104.0 jit_solution(16752999759038640327)
XLA Ops:
  0.6 99.7 %layer.1 = (bf16[128,3584]{1,0:T(8,128)(2,1)}, bf16[128,3584]{1,0:T(8,128)(2,1)}) custom-call(bf16[128,3584]{1,0:T(8,128)(2,1)} %tok.1, f32[3584]{0:T(1024)} %gain.3, bf16[3,1792,640]{2,1,0:T(8,128)(2,1)} %dense_hbm.1, bf16[1,2,3584,640]{3,2,1,0:T(8,128)(2,1)} %gate_up_hbm.1, bf16[1,3584,640]{2,1,0:T(8,128)(2,1)} %down_hbm.1, s32[2,128]{1,0:T(2,128)} %bitcast.2, ...), custom_call_target="tpu_custom_call" | custom-call | tf_op jit(solution)/shard_map/layer/pallas_call | solution.py:459
  100.4 3.7 %finish.1 = (bf16[128,3584]{1,0:T(8,128)(2,1)}, bf16[128,3584]{1,0:T(8,128)(2,1)}) custom-call(bf16[128,3584]{1,0:T(8,128)(2,1)} %tok.1, f32[3584]{0:T(1024)} %gain.3, bf16[128,3584]{1,0:T(8,128)(2,1)} %grad.1, bf16[128,3584]{1,0:T(8,128)(2,1)} %get-tuple-element.4.total_g, bf16[128,3584]{1,0:T(8,128)(2,1)} %get-tuple-element.5.layer_in), custom_call_target="tpu_custom_call" | custom-call | tf_op jit(solution)/shard_map/finish/pallas_call | solution.py:531

commit v5 on v4

--- a/solution.py
+++ b/solution.py
@@ -20,7 +20,7 @@
 RING_G = 768
 DIRECT_G = D - TP * RING_G
 HALF = D // 2
-PARTS_O = ((0, 896), (896, 896), (1792, 896), (2688, 896))
+PARTS_O = ((0, 640), (640, 1024), (1664, 1024), (2688, 896))
 BLOCK = 256
 WHOLE_G = D - TP * BLOCK
 PARTS_G = ((0, 768), (768, 768), (1536, 640), (2176, WHOLE_G - 2176))
@@ -406,8 +406,8 @@
 
     combine_o(2)
     reduce_o(1)
+    merge()
     combine_o(3)
-    merge()
     reduce_o(2)
     reduce_o(3)
     combine_g(0)

time: 104 us -> 104 us (level)
  no operation moved by 1% of the time
where the time goes in v5:
time: 104 us
  Pallas kernels  103 us (99%)
    pallas_call x1, Pallas kernels, body(): pl.pallas_call(kernel, name='layer', out_shape=[row_shape, row_shape], in...  99.7 us
    pallas_call x1, Pallas kernels, body(): pl.pallas_call(finish, name='finish', grid=(2,), out_shape=[row_shape, ro...  3.65 us

profile of v5, /device:TPU:0, one launch (start us, length us, event | category | flops | bytes accessed | tf_op | source)
XLA Modules:
  0.0 104.0 jit_solution(4785718896473281239)
XLA Ops:
  0.6 99.7 %layer.1 = (bf16[128,3584]{1,0:T(8,128)(2,1)}, bf16[128,3584]{1,0:T(8,128)(2,1)}) custom-call(bf16[128,3584]{1,0:T(8,128)(2,1)} %tok.1, f32[3584]{0:T(1024)} %gain.3, bf16[3,1792,640]{2,1,0:T(8,128)(2,1)} %dense_hbm.1, bf16[1,2,3584,640]{3,2,1,0:T(8,128)(2,1)} %gate_up_hbm.1, bf16[1,3584,640]{2,1,0:T(8,128)(2,1)} %down_hbm.1, s32[2,128]{1,0:T(2,128)} %bitcast.2, ...), custom_call_target="tpu_custom_call" | custom-call | tf_op jit(solution)/shard_map/layer/pallas_call | solution.py:459
  100.4 3.7 %finish.1 = (bf16[128,3584]{1,0:T(8,128)(2,1)}, bf16[128,3584]{1,0:T(8,128)(2,1)}) custom-call(bf16[128,3584]{1,0:T(8,128)(2,1)} %tok.1, f32[3584]{0:T(1024)} %gain.3, bf16[128,3584]{1,0:T(8,128)(2,1)} %grad.1, bf16[128,3584]{1,0:T(8,128)(2,1)} %get-tuple-element.4.total_g, bf16[128,3584]{1,0:T(8,128)(2,1)} %get-tuple-element.5.layer_in), custom_call_target="tpu_custom_call" | custom-call | tf_op jit(solution)/shard_map/finish/pallas_call | solution.py:531
